TPU v7x, 128 devices: a whole 4x4x4 slice. The times are simulated.
128 devices in a mesh: gx: 32 (over x, z_hi, y), gy: 4 (over z_lo, core).
Axes of the slice: x: 4, y: 4, z: 4 (z_hi: 2, z_lo: 2; z = z_hi * 2 + z_lo), core: 2. Of those that a mesh axis runs over, the one named last changes fastest.
Arguments:
- nodes: bfloat16 [64, 8, 32, 128], P('gx', 'gy'), may hold values from -6 to 6
- edges: bfloat16 [64, 8, 32, 64, 128], P('gx', 'gy'), may hold values from -6 to 6
- nbr_index: int32 [64, 8, 32, 64], P('gx', 'gy'), may hold values from 0 to 511, as said below
- nbr_mask: int32 [64, 8, 32, 64], P('gx', 'gy'), may hold values from 0 to 1, as said below
- edge_w1: bfloat16 [2, 384, 128], replicated, may hold values from -0.3125 to 0.3125
- edge_b1: float32 [2, 128], replicated, may hold values from -3 to 3
- edge_w2: bfloat16 [2, 128, 128], replicated, may hold values from -0.5 to 0.5
- edge_b2: float32 [2, 128], replicated, may hold values from -3 to 3
- edge_w3: bfloat16 [2, 128, 128], replicated, may hold values from -0.5 to 0.5
- edge_b3: float32 [2, 128], replicated, may hold values from -3 to 3
- edge_gain: float32 [2, 128], replicated, may hold values from 0.25 to 1.75
- edge_shift: float32 [2, 128], replicated, may hold values from -3 to 3
- node_w1: bfloat16 [2, 256, 128], replicated, may hold values from -0.375 to 0.375
- node_b1: float32 [2, 128], replicated, may hold values from -3 to 3
- node_w2: bfloat16 [2, 128, 128], replicated, may hold values from -0.5 to 0.5
- node_b2: float32 [2, 128], replicated, may hold values from -3 to 3
- node_w3: bfloat16 [2, 128, 128], replicated, may hold values from -0.5 to 0.5
- node_b3: float32 [2, 128], replicated, may hold values from -3 to 3
- node_gain: float32 [2, 128], replicated, may hold values from 0.25 to 1.75
- node_shift: float32 [2, 128], replicated, may hold values from -3 to 3
- ct_nodes: bfloat16 [64, 8, 32, 128], P('gx', 'gy'), may hold values from -6 to 6
- ct_edges: bfloat16 [64, 8, 32, 64, 128], P('gx', 'gy'), may hold values from -6 to 6
Outputs:
- nodes_out: bfloat16 [64, 8, 32, 128], P('gx', 'gy')
- edges_out: bfloat16 [64, 8, 32, 64, 128], P('gx', 'gy')
- grad_nodes: float32 [64, 8, 32, 128], P('gx', 'gy')
- grad_edges: float32 [64, 8, 32, 64, 128], P('gx', 'gy')
- grad_edge_w1: float32 [2, 384, 128], replicated
- grad_edge_b1: float32 [2, 128], replicated
- grad_edge_w2: float32 [2, 128, 128], replicated
- grad_edge_b2: float32 [2, 128], replicated
- grad_edge_w3: float32 [2, 128, 128], replicated
- grad_edge_b3: float32 [2, 128], replicated
- grad_edge_gain: float32 [2, 128], replicated
- grad_edge_shift: float32 [2, 128], replicated
- grad_node_w1: float32 [2, 256, 128], replicated
- grad_node_b1: float32 [2, 128], replicated
- grad_node_w2: float32 [2, 128, 128], replicated
- grad_node_b2: float32 [2, 128], replicated
- grad_node_w3: float32 [2, 128, 128], replicated
- grad_node_b3: float32 [2, 128], replicated
- grad_node_gain: float32 [2, 128], replicated
- grad_node_shift: float32 [2, 128], replicated
Inputs may be any that keep to these rules, and one draw needn't show every extreme that they name: `nbr_index`: every slot names a particle slot of the 3 x 3 cells around the receiver's cell; both ends of the range are named on every device. `nbr_mask`: the live slots of a particle are its first c slots, 1 <= c <= 60; on every device some particle has c = 60 and some particle has c = 1.
All inputs are finite; a program needn't handle non-finite values.
Results may differ from a plain program's by a relative error of at most 0.035.
Values may be sent and summed in bfloat16 or wider, within the bound.
A program may use at most 64 MiB of HBM per device.

v0:
```python
import functools

import jax
import jax.numpy as jnp
from jax import lax
from jax.experimental import pallas as pl
from jax.experimental.pallas import tpu as pltpu
from jax.sharding import PartitionSpec as P

EPS = 1e-05
BF = jnp.bfloat16
F32 = jnp.float32
MESH = pl.DeviceIdType.MESH

D = 128
ROWS = 8192
CELL = 2048
SUB = 4
PARTS = 128

DIRS = tuple((dx, dy) for dx in (-1, 0, 1) for dy in (-1, 0, 1) if (dx, dy) != (0, 0))
PLANE = tuple((dx, dy) for dx in range(4) for dy in range(4) if (dx, dy) != (0, 0))
COLUMN = tuple((dz, dg) for dz in range(2) for dg in range(4) if (dz, dg) != (0, 0))

CH1 = 112
CH0 = 48
EDGE_W1, EDGE_W2, EDGE_W3 = 0, 384, 512
NODE_W1, NODE_W2, NODE_W3 = 640, 896, 1024
NODE0 = 1152
VEC1 = 1664
VEC0 = 640


def dot(a, b):
    return jnp.dot(a, b, preferred_element_type=F32)


def dot_nt(a, b):
    return lax.dot_general(a, b, (((1,), (1,)), ((), ())), preferred_element_type=F32)


def dot_tn(a, b):
    return lax.dot_general(a, b, (((0,), (0,)), ((), ())), preferred_element_type=F32)


def iota(shape, dim):
    return lax.broadcasted_iota(jnp.int32, shape, dim)


def silu_parts(half):
    wide = 1.0 + jnp.tanh(half)
    act = half * wide
    slope = wide * (0.5 + half - 0.5 * act)
    return act, slope


def rows_of(start, count):
    return pl.ds(pl.multiple_of(start, count), count)


def partial_rows(x):
    return jnp.sum(x.reshape(-1, 8, D), 0)


def column_sum(x):
    return jnp.sum(x, 0, keepdims=True)


def span(step, low, high, both):
    return low if step < 0 else (high if step > 0 else both)


class Sum:
    def __init__(self, chunk, refs, place):
        self.chunk = chunk
        self.src, self.part, self.col, self.out = refs[:4]
        self.send1, self.recv1, self.send2, self.recv2, self.send3, self.recv3 = refs[4:]
        self.gx, self.gy = place
        self.x, self.z, self.y = self.gx // 8, (self.gx // 4) % 2, self.gx % 4
        self.me = self.x * 4 + self.y
        self.mine = self.z * 4 + self.gy

    def plane_copy(self, k, dx, dy, src, dst, send, recv, slot):
        px, py = (self.x + dx) % 4, (self.y + dy) % 4
        return pltpu.make_async_remote_copy(
            src_ref=src,
            dst_ref=dst,
            send_sem=send.at[k],
            recv_sem=recv.at[slot],
            device_id=((px * 2 + self.z) * 4 + py, self.gy),
            device_id_type=MESH,
        )

    def rows(self, index):
        return pl.ds(pl.multiple_of(index * self.chunk, 16), self.chunk)

    def scatter_start(self):
        for k, (dx, dy) in enumerate(PLANE):
            peer = ((self.x + dx) % 4) * 4 + (self.y + dy) % 4
            self.plane_copy(
                k, dx, dy, self.src.at[self.rows(peer)], self.part.at[self.me], self.send1, self.recv1, self.me
            ).start()
        self.part[self.me] = self.src[self.rows(self.me), :]

    def scatter_finish(self):
        for k, (dx, dy) in enumerate(PLANE):
            peer = ((self.x - dx) % 4) * 4 + (self.y - dy) % 4
            copy = self.plane_copy(
                k, dx, dy, self.src.at[self.rows(peer)], self.part.at[peer], self.send1, self.recv1, peer
            )
            copy.wait_send()
            copy.wait_recv()
        total = self.part[0].astype(F32)
        for k in range(1, 16):
            total = total + self.part[k].astype(F32)
        self.col[self.mine] = total.astype(BF)

    def column_copy(self, k, dz, dg, slot):
        pz, pg = (self.z + dz) % 2, (self.gy + dg) % 4
        return pltpu.make_async_remote_copy(
            src_ref=self.col.at[self.mine],
            dst_ref=self.col.at[slot],
            send_sem=self.send2.at[k],
            recv_sem=self.recv2.at[slot],
            device_id=((self.x * 2 + pz) * 4 + self.y, pg),
            device_id_type=MESH,
        )

    def column_start(self):
        for k, (dz, dg) in enumerate(COLUMN):
            self.column_copy(k, dz, dg, self.mine).start()

    def column_finish(self):
        for k, (dz, dg) in enumerate(COLUMN):
            peer = ((self.z - dz) % 2) * 4 + (self.gy - dg) % 4
            copy = self.column_copy(k, dz, dg, peer)
            copy.wait_send()
            copy.wait_recv()
        total = self.col[0].astype(F32)
        for k in range(1, 8):
            total = total + self.col[k].astype(F32)
        self.out[self.rows(self.me), :] = total.astype(BF)

    def gather_start(self):
        own = self.out.at[self.rows(self.me)]
        for k, (dx, dy) in enumerate(PLANE):
            self.plane_copy(k, dx, dy, own, own, self.send3, self.recv3, self.me).start()

    def gather_finish(self):
        for k, (dx, dy) in enumerate(PLANE):
            peer = ((self.x - dx) % 4) * 4 + (self.y - dy) % 4
            landing = self.out.at[self.rows(peer)]
            copy = self.plane_copy(k, dx, dy, landing, landing, self.send3, self.recv3, peer)
            copy.wait_send()
            copy.wait_recv()


def main_kernel(*refs):
    (
        nodes, edges, index, mask,
        ew1, eb1, ew2, eb2, ew3, eb3, egain, eshift,
        nw1, nb1, nw2, nb2, nw3, nb3, ngain, nshift,
        ct_nodes, ct_edges,
        nodes_out, edges_out, grad_nodes, grad_edges, sum1_out, sum0_out,
        onehot, e0, e1, e2, ct,
        a1_0, s1_0, a2_0, s2_0, n_0, r_0,
        a1_1, s1_1, a2_1, s2_1, n_1, r_1,
        ge, live_count,
        tab, wbig, w2half, w3mid, w1et, w2t, w3t, averager,
        msum, gm, tt, dw2, dw3, sums,
        sender_sum, sender_low, receiver_sum, rim_in,
        nm, nc1, nc2, nsl1, nsl2, nnorm, ninv, gz1_buf, gh_buf,
        src1, part1, col1, src0, part0, col0,
        in_sem, out_sem, halo_send, halo_recv, rim_send, rim_recv,
        *sum_sems,
    ) = refs
    gx, gy = lax.axis_index("gx"), lax.axis_index("gy")
    sum1 = Sum(CH1, (src1, part1, col1, sum1_out, *sum_sems[:6]), (gx, gy))
    sum0 = Sum(CH0, (src0, part0, col0, sum0_out, *sum_sems[6:]), (gx, gy))
    kept = ((a1_0, s1_0, a2_0, s2_0, n_0, r_0), (a1_1, s1_1, a2_1, s2_1, n_1, r_1))
    edge_in = (e0, e1, e2)

    def neighbour(dx, dy):
        return (lax.rem(gx + dx + 32, 32), lax.rem(gy + dy + 4, 4))

    def load(ref, scratch, which, t):
        s = rows_of(t * CELL, CELL)
        return pltpu.make_async_copy(ref.at[s], scratch.at[s], in_sem.at[which, t])

    for t in range(4):
        load(edges, e0, 0, t).start()

    barrier = pltpu.get_barrier_semaphore()
    x, z, y = sum1.x, sum1.z, sum1.y
    partners = [neighbour(dx, dy) for dx, dy in DIRS]
    partners += [(((x + dx) % 4 * 2 + z) * 4 + (y + dy) % 4, gy) for dx, dy in PLANE]
    partners += [((x * 2 + (z + dz) % 2) * 4 + y, (gy + dg) % 4) for dz, dg in COLUMN]
    for partner in partners:
        pl.semaphore_signal(barrier, inc=1, device_id=partner, device_id_type=MESH)
    pl.semaphore_wait(barrier, len(partners))

    def halo_copy(layer, k):
        dx, dy = DIRS[k]
        src = tab.at[layer, span(dx, 1, 2, pl.ds(1, 2)), span(dy, 1, 2, pl.ds(1, 2))]
        dst = tab.at[layer, span(dx, 3, 0, pl.ds(1, 2)), span(dy, 3, 0, pl.ds(1, 2))]
        return pltpu.make_async_remote_copy(
            src_ref=src,
            dst_ref=dst,
            send_sem=halo_send.at[layer, k],
            recv_sem=halo_recv.at[layer, k],
            device_id=neighbour(dx, dy),
            device_id_type=MESH,
        )

    def halo_start(layer, latents):
        for cell in range(4):
            tab[layer, 1 + cell // 2, 1 + cell % 2] = latents[32 * cell : 32 * cell + 32]
        for k in range(8):
            halo_copy(layer, k).start()

    def halo_finish(layer):
        for k in range(8):
            copy = halo_copy(layer, k)
            copy.wait_send()
            copy.wait_recv()
        blank_row = jnp.zeros((4, 32, D), BF)
        for edge, at in ((0, 0), (31, 3)):

            @pl.when(gx == edge)
            def _():
                tab[layer, at] = blank_row

        for edge, at in ((0, 0), (3, 3)):

            @pl.when(gy == edge)
            def _():
                for a in range(4):
                    tab[layer, a, at] = blank_row[0]

    halo_start(0, nodes[...])
    for t in range(4):
        load(ct_edges, ct, 1, t).start()

    averager[...] = jnp.full((D, D), 1.0 / D, BF)
    for layer in range(2):
        w2half[layer] = (0.5 * ew2[layer].astype(F32)).astype(BF)
        w3 = ew3[layer].astype(F32)
        w3mid[layer] = (w3 - jnp.mean(w3, -1, keepdims=True)).astype(BF)
        w3t[layer] = ew3[layer].T
        w2t[layer] = ew2[layer].T
        w1et[layer] = ew1[layer, 2 * D : 3 * D, :].T
    sums[...] = jnp.zeros_like(sums)
    tt[...] = jnp.zeros_like(tt)
    dw2[...] = jnp.zeros_like(dw2)
    dw3[...] = jnp.zeros_like(dw3)

    count = jnp.sum(mask[...].astype(F32), -1, keepdims=True)
    live_count[...] = jnp.broadcast_to(count, (PARTS, D))
    cell_of = iota((PARTS, 64), 0) // 32
    place = index[...] - (cell_of // 2) * 128 - (cell_of % 2) * 32
    place = (place // 128) * 96 + place % 128
    dead = mask[...] == 0
    high = jnp.where(dead, 127, place // 16)
    low = jnp.where(dead, 0, place % 16)
    digits = jnp.concatenate([high, low], 1).astype(F32).astype(BF)
    spread = jnp.where(iota((D, D), 0) < 64, 16.0, 1.0).astype(BF)

    def onehot_step(t, carry):
        row = iota((CELL, D), 0)
        lane = iota((CELL, D), 1)
        pick = jnp.where(lane == t * 32 + row // 64, 1.0, 0.0).astype(BF)
        spread_out = dot(pick, digits)
        own = jnp.where(lane % 64 == row % 64, spread_out, 0.0).astype(BF)
        found = dot(own, spread).astype(jnp.int32)
        s = rows_of(t * CELL, CELL)
        onehot[s, 0:128] = jnp.where(found == lane, 1.0, 0.0).astype(BF)
        onehot[s, 128:256] = jnp.where(found == lane + 128, 1.0, 0.0).astype(BF)
        fixed = (lane == 32 + row // 64) | (lane == 64) | (lane == 65)
        onehot[s, 256:384] = jnp.where((found == lane + 256) | fixed, 1.0, 0.0).astype(BF)
        return carry

    lax.fori_loop(0, 4, onehot_step, 0)

    def prepare(layer):
        senders = dot(tab[layer].reshape(512, D), ew1[layer, D : 2 * D, :])
        senders = (0.5 * senders).astype(BF).reshape(4, 4, 32, D)
        own = jnp.concatenate([tab[layer, 1 + c // 2, 1 + c % 2] for c in range(4)], 0)
        receivers = (0.5 * dot(own, ew1[layer, 0:D, :])).astype(BF)
        bias = 0.5 * eb1[layer : layer + 1, :]
        bias_high = bias.astype(BF).astype(F32)
        at = iota((64, D), 0)
        bias_rows = jnp.where(at == 0, bias_high, jnp.where(at == 1, bias - bias_high, 0.0)).astype(BF)
        edge_rows = (0.5 * ew1[layer, 2 * D : 3 * D, :].astype(F32)).astype(BF)
        for c in range(4):
            i, j = c // 2, c % 2
            for a in range(3):
                wbig[c, 96 * a : 96 * a + 96, :] = senders[i + a, j : j + 3].reshape(96, D)
            wbig[c, 288:320, :] = receivers[32 * c : 32 * c + 32]
            wbig[c, 320:384, :] = bias_rows
            wbig[c, 384:512, :] = edge_rows

    step = CELL // SUB
    per = step // 64

    def live_of(p):
        slot = iota((per, 64, D), 1).astype(F32)
        return slot < live_count[p, :][:, None, :]

    def forward(layer):
        a1, s1, a2, s2, nn, rr = kept[layer]
        e_in, e_out = edge_in[layer], edge_in[layer + 1]
        b2 = 0.5 * eb2[layer : layer + 1, :]
        b3 = eb3[layer : layer + 1, :]
        b3 = b3 - jnp.mean(b3, -1, keepdims=True)
        gain, shift = egain[layer : layer + 1, :], eshift[layer : layer + 1, :]

        def body(t, carry):
            if layer == 0:
                load(edges, e0, 0, t).wait()
            groups = [rows_of(t * CELL + g * step, step) for g in range(SUB)]
            ones = [dot(jnp.concatenate([onehot[s, :], e_in[s, :]], 1), wbig[t]) for s in groups]
            first = []
            for s, half in zip(groups, ones):
                act, slope = silu_parts(half)
                a1[s, :] = act.astype(BF)
                s1[s, :] = slope.astype(BF)
                first.append(act.astype(BF))
            twos = [dot(act, w2half[layer]) + b2 for act in first]
            second = []
            for s, half in zip(groups, twos):
                act, slope = silu_parts(half)
                a2[s, :] = act.astype(BF)
                s2[s, :] = slope.astype(BF)
                second.append(act.astype(BF))
            mids = [dot(act, w3mid[layer]) + b3 for act in second]
            spreads = [dot((mid * mid).astype(BF), averager[...]) for mid in mids]
            for g, (s, mid, var) in enumerate(zip(groups, mids, spreads)):
                inverse = lax.rsqrt(var + EPS)
                normed = mid * inverse
                nn[s, :] = normed.astype(BF)
                rr[s, :] = inverse.astype(BF)
                update = (normed * gain + shift).reshape(per, 64, D)
                p = rows_of(t * 32 + g * per, per)
                live = live_of(p)
                new = e_in[s, :].astype(F32).reshape(per, 64, D) + jnp.where(live, update, 0.0)
                new = new.astype(BF)
                e_out[s, :] = new.reshape(step, D)
                msum[p, :] = jnp.sum(jnp.where(live, new.astype(F32), 0.0), 1)
            if layer == 1:
                s = rows_of(t * CELL, CELL)
                pltpu.make_async_copy(e2.at[s], edges_out.at[s], out_sem.at[0, t]).start()
            return carry

        lax.fori_loop(0, 4, body, 0)

    def node_forward(layer, h):
        m = msum[...].astype(BF)
        z1 = dot(h, nw1[layer, 0:D, :]) + dot(m, nw1[layer, D : 2 * D, :]) + nb1[layer : layer + 1, :]
        c1, slope1 = silu_parts(0.5 * z1)
        c1 = c1.astype(BF)
        z2 = dot(c1, nw2[layer]) + nb2[layer : layer + 1, :]
        c2, slope2 = silu_parts(0.5 * z2)
        c2 = c2.astype(BF)
        z3 = dot(c2, nw3[layer]) + nb3[layer : layer + 1, :]
        mid = z3 - jnp.mean(z3, -1, keepdims=True)
        inverse = lax.rsqrt(jnp.mean(mid * mid, -1, keepdims=True) + EPS)
        normed = mid * inverse
        nm[layer], nc1[layer], nc2[layer] = m, c1, c2
        nsl1[layer], nsl2[layer], nnorm[layer] = slope1, slope2, normed
        ninv[layer] = jnp.broadcast_to(inverse, (PARTS, D))
        update = normed * ngain[layer : layer + 1, :] + nshift[layer : layer + 1, :]
        return (h.astype(F32) + update).astype(BF)

    def node_backward(layer, h, gh, dst, row, vec):
        normed = nnorm[layer]
        q = gh * ngain[layer : layer + 1, :]
        inner = q - jnp.mean(q, -1, keepdims=True) - normed * jnp.mean(q * normed, -1, keepdims=True)
        gz3 = ninv[layer] * inner
        low3 = gz3.astype(BF)
        gz2 = dot_nt(low3, nw3[layer]) * nsl2[layer]
        low2 = gz2.astype(BF)
        gz1 = dot_nt(low2, nw2[layer]) * nsl1[layer]
        low1 = gz1.astype(BF)
        gz1_buf[...] = low1
        gm[...] = dot_nt(low1, nw1[layer, D : 2 * D, :])
        dst[row : row + 128, :] = dot_tn(h, low1).astype(BF)
        dst[row + 128 : row + 256, :] = dot_tn(nm[layer], low1).astype(BF)
        dst[row + 256 : row + 384, :] = dot_tn(nc1[layer], low2).astype(BF)
        dst[row + 384 : row + 512, :] = dot_tn(nc2[layer], low3).astype(BF)
        vec.extend([column_sum(gz1), column_sum(gz2), column_sum(gz3), column_sum(gh * normed), column_sum(gh)])

    def backward(layer):
        a1, s1, a2, s2, nn, rr = kept[layer]
        e_in = edge_in[layer]
        gain = egain[layer : layer + 1, :]

        def body(t, carry):
            if layer == 1:
                load(ct_edges, ct, 1, t).wait()
            groups = [rows_of(t * CELL + g * step, step) for g in range(SUB)]
            firsts = []
            for g, s in enumerate(groups):
                p = rows_of(t * 32 + g * per, per)
                live = live_of(p)
                old = ct[s, :].astype(F32) if layer == 1 else ge[s, :]
                total = old.reshape(per, 64, D) + jnp.where(live, gm[p, :][:, None, :], 0.0)
                gy_ = jnp.where(live, total, 0.0).reshape(step, D)
                normed = nn[s, :].astype(F32)
                q = gy_ * gain
                qn = q * normed
                mean_q = dot(q.astype(BF), averager[...])
                mean_qn = dot(qn.astype(BF), averager[...])
                firsts.append((total.reshape(step, D), gy_, q, qn, normed, mean_q, mean_qn))
            g3 = [
                rr[s, :].astype(F32) * (f[2] - f[5] - f[4] * f[6]) for s, f in zip(groups, firsts)
            ]
            low3 = [g.astype(BF) for g in g3]
            g2 = [dot(g, w3t[layer]) * s2[s, :].astype(F32) for s, g in zip(groups, low3)]
            low2 = [g.astype(BF) for g in g2]
            low1 = [(dot(g, w2t[layer]) * s1[s, :].astype(F32)).astype(BF) for s, g in zip(groups, low2)]
            for s, g, f in zip(groups, low1, firsts):
                ge[s, :] = f[0] + dot(g, w1et[layer])
            sums[layer, 0] += sum(partial_rows(f[3]) for f in firsts)
            sums[layer, 1] += sum(partial_rows(f[1]) for f in firsts)
            sums[layer, 2] += sum(partial_rows(g) for g in g3)
            sums[layer, 3] += sum(partial_rows(g) for g in g2)
            s = rows_of(t * CELL, CELL)
            left = jnp.concatenate([onehot[s, :], e_in[s, :]], 1)
            tt[layer, t] = dot_tn(jnp.concatenate(low1, 0), left)
            dw2[layer] += dot_tn(jnp.concatenate(low2, 0), a1[s, :])
            dw3[layer] += dot_tn(jnp.concatenate(low3, 0), a2[s, :])
            if layer == 0:
                pltpu.make_async_copy(ge.at[s], grad_edges.at[s], out_sem.at[1, t]).start()

                @pl.when(t == 1)
                def _():
                    sum1.scatter_finish()
                    sum1.column_start()

                @pl.when(t == 3)
                def _():
                    sum1.column_finish()
                    sum1.gather_start()

            return carry

        lax.fori_loop(0, 4, body, 0)

    def rim_copy(layer, k):
        dx, dy = DIRS[k]
        src = sender_low.at[layer, span(dx, 0, 3, pl.ds(1, 2)), span(dy, 0, 3, pl.ds(1, 2))]
        dst = rim_in.at[layer, k, 0] if dx != 0 and dy != 0 else rim_in.at[layer, k]
        return pltpu.make_async_remote_copy(
            src_ref=src,
            dst_ref=dst,
            send_sem=rim_send.at[layer, k],
            recv_sem=rim_recv.at[layer, k],
            device_id=neighbour(dx, dy),
            device_id_type=MESH,
        )

    def rims_start(layer):
        sender_sum[...] = jnp.zeros_like(sender_sum)
        for c in range(4):
            i, j = c // 2, c % 2
            by_row = tt[layer, c, :, 0:384].T
            for a in range(3):
                piece = by_row[96 * a : 96 * a + 96].reshape(3, 32, D)
                for b in range(3):
                    sender_sum[i + a, j + b] += piece[b]
            receiver_sum[32 * c : 32 * c + 32, :] = by_row[288:320]
            sums[layer, 4] += jnp.where(iota((8, D), 0) == 0, by_row[320:328], 0.0)
        sender_low[layer] = sender_sum[...].astype(BF)
        for k in range(8):
            rim_copy(layer, k).start()

    def edge_grads(layer, h, dst, row, vec):
        dst[row : row + 128, :] = dot_tn(h, receiver_sum[...].astype(BF)).astype(BF)
        senders = dot_tn(tab[layer].reshape(512, D), sender_low[layer].reshape(512, D))
        dst[row + 128 : row + 256, :] = senders.astype(BF)
        by_edge = sum(tt[layer, c, :, 384:512] for c in range(4))
        dst[row + 256 : row + 384, :] = by_edge.T.astype(BF)
        dst[row + 384 : row + 512, :] = dw2[layer].T.astype(BF)
        dst[row + 512 : row + 640, :] = dw3[layer].T.astype(BF)
        s = [column_sum(sums[layer, k]) for k in range(5)]
        vec.extend([s[4], s[3], s[2], s[0] / egain[layer : layer + 1, :], s[1]])

    def rims_finish(layer, gh):
        for k in range(8):
            copy = rim_copy(layer, k)
            copy.wait_send()
            copy.wait_recv()
        own = [sender_sum[1 + c // 2, 1 + c % 2] for c in range(4)]
        for k, (dx, dy) in enumerate(DIRS):
            fits = jnp.bool_(True)
            if dx != 0:
                fits = gx != (0 if dx > 0 else 31)
            if dy != 0:
                fits = fits & (gy != (0 if dy > 0 else 3))
            scale = jnp.where(fits, 1.0, 0.0)
            cells = [
                (i, j)
                for i in ((0, 1) if dx == 0 else ((0,) if dx > 0 else (1,)))
                for j in ((0, 1) if dy == 0 else ((0,) if dy > 0 else (1,)))
            ]
            for at, (i, j) in enumerate(cells):
                own[2 * i + j] = own[2 * i + j] + scale * rim_in[layer, k, at].astype(F32)
        own = jnp.concatenate(own, 0).astype(BF)
        gh = gh + dot_nt(gz1_buf[...], nw1[layer, 0:D, :])
        gh = gh + dot_nt(receiver_sum[...].astype(BF), ew1[layer, 0:D, :])
        return gh + dot_nt(own, ew1[layer, D : 2 * D, :])

    def put_vectors(dst, row, vec):
        at = iota((16, D), 0)
        block = jnp.zeros((16, D), F32)
        for k, v in enumerate(vec):
            block = jnp.where(at == k, v, block)
        dst[row : row + 16, :] = block.astype(BF)

    halo_finish(0)
    prepare(0)
    forward(0)
    h1 = node_forward(0, nodes[...])
    halo_start(1, h1)
    halo_finish(1)
    prepare(1)
    forward(1)
    own1 = jnp.concatenate([tab[1, 1 + c // 2, 1 + c % 2] for c in range(4)], 0)
    nodes_out[...] = node_forward(1, own1)

    vec1 = []
    gh_buf[...] = ct_nodes[...].astype(F32)
    src1[VEC1 + 16 :, :] = jnp.zeros((CH1 * 16 - VEC1 - 16, D), BF)
    src0[VEC0 + 16 :, :] = jnp.zeros((CH0 * 16 - VEC0 - 16, D), BF)
    node_backward(1, own1, gh_buf[...], src1, NODE_W1, vec1)
    backward(1)
    rims_start(1)
    edge_grads(1, own1, src1, EDGE_W1, vec1)
    gh_buf[...] = rims_finish(1, gh_buf[...])

    node_backward(0, nodes[...], gh_buf[...], src1, NODE0, vec1)
    put_vectors(src1, VEC1, vec1)
    sum1.scatter_start()
    backward(0)
    rims_start(0)
    vec0 = []
    edge_grads(0, nodes[...], src0, EDGE_W1, vec0)
    put_vectors(src0, VEC0, vec0)
    sum0.scatter_start()
    grad_nodes[...] = rims_finish(0, gh_buf[...])
    sum0.scatter_finish()
    sum0.column_start()
    sum1.gather_finish()
    sum0.column_finish()
    sum0.gather_start()
    for t in range(4):
        s = rows_of(t * CELL, CELL)
        pltpu.make_async_copy(e2.at[s], edges_out.at[s], out_sem.at[0, t]).wait()
        pltpu.make_async_copy(ge.at[s], grad_edges.at[s], out_sem.at[1, t]).wait()
    sum0.gather_finish()


def unpack_kernel(sum1, sum0, *outs):
    w1, b1, w2, b2, w3, b3, gain, shift, v1, c1, v2, c2, v3, c3, ngain, nshift = outs

    def put(ref, layer, buffer, row):
        height = ref.shape[1]
        ref[layer] = buffer[row : row + height, :].astype(F32)

    for layer, buffer, row in ((1, sum1, 0), (0, sum0, 0)):
        put(w1, layer, buffer, row + EDGE_W1)
        put(w2, layer, buffer, row + EDGE_W2)
        put(w3, layer, buffer, row + EDGE_W3)
    for layer, row in ((1, 0), (0, NODE0 - NODE_W1)):
        put(v1, layer, sum1, row + NODE_W1)
        put(v2, layer, sum1, row + NODE_W2)
        put(v3, layer, sum1, row + NODE_W3)
    first = sum1[VEC1 : VEC1 + 16, :].astype(F32)
    second = sum0[VEC0 : VEC0 + 16, :].astype(F32)
    for k, ref in enumerate((c1, c2, c3, ngain, nshift)):
        ref[1:2, :] = first[k : k + 1]
        ref[0:1, :] = first[10 + k : 11 + k]
    for k, ref in enumerate((b1, b2, b3, gain, shift)):
        ref[1:2, :] = first[5 + k : 6 + k]
        ref[0:1, :] = second[k : k + 1]


def per_device(nodes, edges, nbr_index, nbr_mask, *rest):
    weights, ct_nodes, ct_edges = rest[:16], rest[16], rest[17]
    vmem = pl.BlockSpec(memory_space=pltpu.VMEM)
    hbm = pl.BlockSpec(memory_space=pl.ANY)
    shape = jax.ShapeDtypeStruct
    big = pltpu.VMEM((ROWS, D), BF)
    node_bf = pltpu.VMEM((2, PARTS, D), BF)
    node_f32 = pltpu.VMEM((2, PARTS, D), F32)
    square = pltpu.VMEM((2, D, D), BF)
    dma = pltpu.SemaphoreType.DMA

    def sum_scratch(chunk):
        return [
            pltpu.VMEM((16 * chunk, D), BF),
            pltpu.VMEM((16, chunk, D), BF),
            pltpu.VMEM((8, chunk, D), BF),
        ]

    scratch = [
        pltpu.VMEM((ROWS, 3 * D), BF),
        big, big, big, big,
        *([big] * 12),
        pltpu.VMEM((ROWS, D), F32),
        pltpu.VMEM((PARTS, D), F32),
        pltpu.VMEM((2, 4, 4, 32, D), BF),
        pltpu.VMEM((4, 4 * D, D), BF),
        square, square, square, square, square,
        pltpu.VMEM((D, D), BF),
        pltpu.VMEM((PARTS, D), F32),
        pltpu.VMEM((PARTS, D), F32),
        pltpu.VMEM((2, 4, D, 4 * D), F32),
        pltpu.VMEM((2, D, D), F32),
        pltpu.VMEM((2, D, D), F32),
        pltpu.VMEM((2, 5, 8, D), F32),
        pltpu.VMEM((4, 4, 32, D), F32),
        pltpu.VMEM((2, 4, 4, 32, D), BF),
        pltpu.VMEM((PARTS, D), F32),
        pltpu.VMEM((2, 8, 2, 32, D), BF),
        node_bf, node_bf, node_bf, node_f32, node_f32, node_f32, node_f32,
        pltpu.VMEM((PARTS, D), BF),
        pltpu.VMEM((PARTS, D), F32),
        *sum_scratch(CH1),
        *sum_scratch(CH0),
        dma((2, 4)), dma((2, 4)), dma((2, 8)), dma((2, 8)), dma((2, 8)), dma((2, 8)),
        *([dma((15,)), dma((16,)), dma((7,)), dma((8,)), dma((15,)), dma((16,))] * 2),
    ]
    nodes_out, edges_out, grad_nodes, grad_edges, sum1, sum0 = pl.pallas_call(
        main_kernel,
        out_shape=(
            shape((PARTS, D), BF),
            shape((ROWS, D), BF),
            shape((PARTS, D), F32),
            shape((ROWS, D), F32),
            shape((16 * CH1, D), BF),
            shape((16 * CH0, D), BF),
        ),
        in_specs=[vmem, hbm] + [vmem] * 19 + [hbm],
        out_specs=(vmem, hbm, vmem, hbm, vmem, vmem),
        scratch_shapes=scratch,
        compiler_params=pltpu.CompilerParams(
            collective_id=0, has_side_effects=True, vmem_limit_bytes=60 * 1024 * 1024
        ),
        name="interaction_layers",
    )(
        nodes.reshape(PARTS, D),
        edges.reshape(ROWS, D),
        nbr_index.reshape(PARTS, 64),
        nbr_mask.reshape(PARTS, 64),
        *weights,
        ct_nodes.reshape(PARTS, D),
        ct_edges.reshape(ROWS, D),
    )
    grads = pl.pallas_call(
        unpack_kernel,
        out_shape=tuple(shape(w.shape, F32) for w in weights),
        in_specs=[vmem, vmem],
        out_specs=(vmem,) * 16,
        name="unpack_sums",
    )(sum1, sum0)
    return (
        nodes_out.reshape(nodes.shape),
        edges_out.reshape(edges.shape),
        grad_nodes.reshape(nodes.shape),
        grad_edges.reshape(edges.shape),
        *grads,
    )


def solution(mesh):
    cells = P("gx", "gy", None, None)
    wide = P("gx", "gy", None, None, None)
    in_specs = (cells, wide, cells, cells) + (P(),) * 16 + (cells, wide)
    out_specs = (cells, wide, cells, wide) + (P(),) * 16
    return jax.shard_map(
        per_device, mesh=mesh, in_specs=in_specs, out_specs=out_specs, check_vma=False
    )
```

profile of v0, /device:TPU:0, one launch (start us, length us, event | category | flops | bytes accessed | tf_op | source)
XLA Modules:
  0.0 96.4 jit_solution(15327808451397894346)
XLA Ops:
  0.7 86.3 %interaction_layers.1 = (bf16[128,128]{1,0:T(8,128)(2,1)}, bf16[8192,128]{1,0:T(8,128)(2,1)}, f32[128,128]{1,0:T(8,128)}, f32[8192,128]{1,0:T(8,128)}, bf16[1792...) custom-call(bf16[128,128]{1,0:T(8,128)(2,1)} %bitcast.17, bf16[8192,128]{1,0:T(8,128)(2,1)} %bitcast.11, s32[128,64]{1,0:T(8,128)} %bitcast.14, ...), custom_call_target="tpu_custom_call" | custom-call | tf_op jit(solution)/shard_map/interaction_layers/pallas_call | solution.py:634
  86.9 2.1 %unpack_sums.1 = (f32[2,384,128]{2,1,0:T(8,128)}, f32[2,128]{1,0:T(2,128)}, f32[2,128,128]{2,1,0:T(8,128)}, f32[2,128]{1,0:T(2,128)}, f32[2,128,128]{2,1,0:T(8,1...) custom-call(bf16[1792,128]{1,0:T(8,128)(2,1)} %get-tuple-element.46., ...), custom_call_target="tpu_custom_call" | custom-call | tf_op jit(solution)/shard_map/unpack_sums/pallas_call | solution.py:660
  89.1 0.0 copy-start.1
  89.1 1.4 %copy.46 = bf16[2,2,32,128]{3,2,1,0:T(8,128)(2,1)} copy(bf16[2,2,32,128]{3,2,1,0:T(8,128)(2,1)} %bitcast.19) | data formatting | bytes 65536
  90.5 0.0 copy-start
  90.5 3.2 %copy.47 = bf16[2,2,32,64,128]{4,3,2,1,0:T(8,128)(2,1)} copy(bf16[2,2,32,64,128]{4,3,2,1,0:T(8,128)(2,1)} %bitcast.13) | data formatting | bytes 4194304
  93.7 0.0 copy-done.1
  93.7 0.6 copy.48
  94.3 0.0 copy-done
  94.4 2.0 %copy.49 = f32[2,2,32,64,128]{4,3,2,1,0:T(8,128)} copy(f32[2,2,32,64,128]{4,3,2,1,0:T(8,128)S(1)} %bitcast.10) | data formatting | bytes 8388608
Async XLA Ops:
  89.1 4.7 %copy-start.1 = (f32[128,128]{1,0:T(8,128)S(1)}, f32[128,128]{1,0:T(8,128)}, u32[]{:S(2)}) copy-start(f32[128,128]{1,0:T(8,128)} %get-tuple-element.44) | copy-start | bytes 196612
  90.5 3.9 %copy-start = (f32[8192,128]{1,0:T(8,128)S(1)}, f32[8192,128]{1,0:T(8,128)}, u32[]{:S(2)}) copy-start(f32[8192,128]{1,0:T(8,128)} %get-tuple-element.45) | copy-start | bytes 12582916
where the time goes:
time: 96.8 us; the launch traced here: 96.4 us
  Pallas kernels  88.4 us (91%)
  local copies, waits for them, and re-layouts  7.29 us (8%)
    pallas_call x1, Pallas kernels, per_device(): pl.pallas_call(main_kernel, out_shape=(shape((PARTS, D), BF), shape((ROWS...  86.3 us
    unnamed x8, local copies, waits for them, and re-layouts  7.29 us
    pallas_call x1, Pallas kernels, per_device(): pl.pallas_call(unpack_kernel, out_shape=tuple((shape(w.shape, F32) for w...  2.13 us

commit v1 on v0

--- a/solution.py
+++ b/solution.py
@@ -22,13 +22,15 @@
 PLANE = tuple((dx, dy) for dx in range(4) for dy in range(4) if (dx, dy) != (0, 0))
 COLUMN = tuple((dz, dg) for dz in range(2) for dg in range(4) if (dz, dg) != (0, 0))
 
-CH1 = 112
+CH1 = 80
+CHN = 32
 CH0 = 48
 EDGE_W1, EDGE_W2, EDGE_W3 = 0, 384, 512
 NODE_W1, NODE_W2, NODE_W3 = 640, 896, 1024
-NODE0 = 1152
-VEC1 = 1664
+VEC1 = 1152
 VEC0 = 640
+FIRST_HALO = ((3, 1), (3, 2), (3, 3), (1, 3), (2, 3))
+OTHER_HALO = ((0, 0), (0, 1), (0, 2), (0, 3), (1, 0), (2, 0), (3, 0))
 
 
 def dot(a, b):
@@ -161,22 +163,23 @@
         ew1, eb1, ew2, eb2, ew3, eb3, egain, eshift,
         nw1, nb1, nw2, nb2, nw3, nb3, ngain, nshift,
         ct_nodes, ct_edges,
-        nodes_out, edges_out, grad_nodes, grad_edges, sum1_out, sum0_out,
-        onehot, e0, e1, e2, ct,
+        nodes_out, e2, grad_nodes, ge, sum1_out, sumn_out, sum0_out,
+        onehot, e0, e1, ct,
         a1_0, s1_0, a2_0, s2_0, n_0, r_0,
         a1_1, s1_1, a2_1, s2_1, n_1, r_1,
-        ge, live_count,
+        live_count,
         tab, wbig, w2half, w3mid, w1et, w2t, w3t, averager,
         msum, gm, tt, dw2, dw3, sums,
         sender_sum, sender_low, receiver_sum, rim_in,
         nm, nc1, nc2, nsl1, nsl2, nnorm, ninv, gz1_buf, gh_buf,
-        src1, part1, col1, src0, part0, col0,
-        in_sem, out_sem, halo_send, halo_recv, rim_send, rim_recv,
+        src1, part1, col1, srcn, partn, coln, src0, part0, col0,
+        in_sem, halo_send, halo_recv, cell_send, cell_recv, rim_send, rim_recv,
         *sum_sems,
     ) = refs
     gx, gy = lax.axis_index("gx"), lax.axis_index("gy")
     sum1 = Sum(CH1, (src1, part1, col1, sum1_out, *sum_sems[:6]), (gx, gy))
-    sum0 = Sum(CH0, (src0, part0, col0, sum0_out, *sum_sems[6:]), (gx, gy))
+    sumn = Sum(CHN, (srcn, partn, coln, sumn_out, *sum_sems[6:12]), (gx, gy))
+    sum0 = Sum(CH0, (src0, part0, col0, sum0_out, *sum_sems[12:]), (gx, gy))
     kept = ((a1_0, s1_0, a2_0, s2_0, n_0, r_0), (a1_1, s1_1, a2_1, s2_1, n_1, r_1))
     edge_in = (e0, e1, e2)
 
@@ -199,45 +202,75 @@
         pl.semaphore_signal(barrier, inc=1, device_id=partner, device_id_type=MESH)
     pl.semaphore_wait(barrier, len(partners))
 
-    def halo_copy(layer, k):
+    def halo_copy(k):
         dx, dy = DIRS[k]
-        src = tab.at[layer, span(dx, 1, 2, pl.ds(1, 2)), span(dy, 1, 2, pl.ds(1, 2))]
-        dst = tab.at[layer, span(dx, 3, 0, pl.ds(1, 2)), span(dy, 3, 0, pl.ds(1, 2))]
+        src = tab.at[0, span(dx, 1, 2, pl.ds(1, 2)), span(dy, 1, 2, pl.ds(1, 2))]
+        dst = tab.at[0, span(dx, 3, 0, pl.ds(1, 2)), span(dy, 3, 0, pl.ds(1, 2))]
         return pltpu.make_async_remote_copy(
             src_ref=src,
             dst_ref=dst,
-            send_sem=halo_send.at[layer, k],
-            recv_sem=halo_recv.at[layer, k],
+            send_sem=halo_send.at[k],
+            recv_sem=halo_recv.at[k],
             device_id=neighbour(dx, dy),
             device_id_type=MESH,
         )
 
-    def halo_start(layer, latents):
+    def clear_outside(layer, places):
+        blank = jnp.zeros((32, D), BF)
+        for outside, dim, at in ((gx == 0, 0, 0), (gx == 31, 0, 3), (gy == 0, 1, 0), (gy == 3, 1, 3)):
+            chosen = [place for place in places if place[dim] == at]
+            if chosen:
+
+                @pl.when(outside)
+                def _():
+                    for a, b in chosen:
+                        tab[layer, a, b] = blank
+
+    def halo_start(latents):
         for cell in range(4):
-            tab[layer, 1 + cell // 2, 1 + cell % 2] = latents[32 * cell : 32 * cell + 32]
+            tab[0, 1 + cell // 2, 1 + cell % 2] = latents[32 * cell : 32 * cell + 32]
         for k in range(8):
-            halo_copy(layer, k).start()
-
-    def halo_finish(layer):
+            halo_copy(k).start()
+
+    def halo_finish():
         for k in range(8):
-            copy = halo_copy(layer, k)
+            copy = halo_copy(k)
             copy.wait_send()
             copy.wait_recv()
-        blank_row = jnp.zeros((4, 32, D), BF)
-        for edge, at in ((0, 0), (31, 3)):
-
-            @pl.when(gx == edge)
-            def _():
-                tab[layer, at] = blank_row
-
-        for edge, at in ((0, 0), (3, 3)):
-
-            @pl.when(gy == edge)
-            def _():
-                for a in range(4):
-                    tab[layer, a, at] = blank_row[0]
-
-    halo_start(0, nodes[...])
+        clear_outside(0, FIRST_HALO + OTHER_HALO)
+
+    def cell_copy(c, k):
+        i, j = c // 2, c % 2
+        dx = 2 * i - 1 if k != 1 else 0
+        dy = 2 * j - 1 if k != 0 else 0
+        a = 3 - 3 * i if k != 1 else 1 + i
+        b = 3 - 3 * j if k != 0 else 1 + j
+        return pltpu.make_async_remote_copy(
+            src_ref=tab.at[1, 1 + i, 1 + j],
+            dst_ref=tab.at[1, a, b],
+            send_sem=cell_send.at[c, k],
+            recv_sem=cell_recv.at[a, b],
+            device_id=neighbour(dx, dy),
+            device_id_type=MESH,
+        )
+
+    def cell_start(c):
+        for k in range(3):
+            cell_copy(c, k).start()
+
+    def cells_arrive(places):
+        for a, b in places:
+            pltpu.make_async_remote_copy(
+                src_ref=tab.at[1, 1, 1],
+                dst_ref=tab.at[1, a, b],
+                send_sem=cell_send.at[0, 0],
+                recv_sem=cell_recv.at[a, b],
+                device_id=neighbour(1, 0),
+                device_id_type=MESH,
+            ).wait_recv()
+        clear_outside(1, places)
+
+    halo_start(nodes[...])
     for t in range(4):
         load(ct_edges, ct, 1, t).start()
 
@@ -249,6 +282,7 @@
         w3t[layer] = ew3[layer].T
         w2t[layer] = ew2[layer].T
         w1et[layer] = ew1[layer, 2 * D : 3 * D, :].T
+    msum[...] = jnp.zeros_like(msum)
     sums[...] = jnp.zeros_like(sums)
     tt[...] = jnp.zeros_like(tt)
     dw2[...] = jnp.zeros_like(dw2)
@@ -281,21 +315,23 @@
 
     lax.fori_loop(0, 4, onehot_step, 0)
 
-    def prepare(layer):
-        senders = dot(tab[layer].reshape(512, D), ew1[layer, D : 2 * D, :])
-        senders = (0.5 * senders).astype(BF).reshape(4, 4, 32, D)
-        own = jnp.concatenate([tab[layer, 1 + c // 2, 1 + c % 2] for c in range(4)], 0)
+    def prepare(layer, cells):
+        base = 1 if cells == (3,) else 0
+        width = 4 - base
+        senders = dot(tab[layer, base:, base:].reshape(width * width * 32, D), ew1[layer, D : 2 * D, :])
+        senders = (0.5 * senders).astype(BF).reshape(width, width, 32, D)
+        own = jnp.concatenate([tab[layer, 1 + c // 2, 1 + c % 2] for c in cells], 0)
         receivers = (0.5 * dot(own, ew1[layer, 0:D, :])).astype(BF)
         bias = 0.5 * eb1[layer : layer + 1, :]
         bias_high = bias.astype(BF).astype(F32)
         at = iota((64, D), 0)
         bias_rows = jnp.where(at == 0, bias_high, jnp.where(at == 1, bias - bias_high, 0.0)).astype(BF)
         edge_rows = (0.5 * ew1[layer, 2 * D : 3 * D, :].astype(F32)).astype(BF)
-        for c in range(4):
-            i, j = c // 2, c % 2
+        for k, c in enumerate(cells):
+            i, j = c // 2 - base, c % 2 - base
             for a in range(3):
                 wbig[c, 96 * a : 96 * a + 96, :] = senders[i + a, j : j + 3].reshape(96, D)
-            wbig[c, 288:320, :] = receivers[32 * c : 32 * c + 32]
+            wbig[c, 288:320, :] = receivers[32 * k : 32 * k + 32]
             wbig[c, 320:384, :] = bias_rows
             wbig[c, 384:512, :] = edge_rows
 
@@ -317,8 +353,10 @@
         def body(t, carry):
             if layer == 0:
                 load(edges, e0, 0, t).wait()
-            groups = [rows_of(t * CELL + g * step, step) for g in range(SUB)]
-            ones = [dot(jnp.concatenate([onehot[s, :], e_in[s, :]], 1), wbig[t]) for s in groups]
+                node_forward(0, jnp.maximum(t - 1, 0))
+            c = t if layer == 0 else 3 - t
+            groups = [rows_of(c * CELL + g * step, step) for g in range(SUB)]
+            ones = [dot(jnp.concatenate([onehot[s, :], e_in[s, :]], 1), wbig[c]) for s in groups]
             first = []
             for s, half in zip(groups, ones):
                 act, slope = silu_parts(half)
@@ -340,21 +378,37 @@
                 nn[s, :] = normed.astype(BF)
                 rr[s, :] = inverse.astype(BF)
                 update = (normed * gain + shift).reshape(per, 64, D)
-                p = rows_of(t * 32 + g * per, per)
+                p = rows_of(c * 32 + g * per, per)
                 live = live_of(p)
                 new = e_in[s, :].astype(F32).reshape(per, 64, D) + jnp.where(live, update, 0.0)
                 new = new.astype(BF)
                 e_out[s, :] = new.reshape(step, D)
                 msum[p, :] = jnp.sum(jnp.where(live, new.astype(F32), 0.0), 1)
-            if layer == 1:
-                s = rows_of(t * CELL, CELL)
-                pltpu.make_async_copy(e2.at[s], edges_out.at[s], out_sem.at[0, t]).start()
+            if layer == 0:
+
+                @pl.when(t > 0)
+                def _():
+                    cell_start(t - 1)
+
+            else:
+
+                @pl.when(t == 0)
+                def _():
+                    cells_arrive(OTHER_HALO)
+                    prepare(1, (0, 1, 2))
+
             return carry
 
         lax.fori_loop(0, 4, body, 0)
 
-    def node_forward(layer, h):
-        m = msum[...].astype(BF)
+    def node_forward(layer, c=None):
+        if c is None:
+            p = pl.ds(0, PARTS)
+            h = jnp.concatenate([tab[layer, 1 + k // 2, 1 + k % 2] for k in range(4)], 0)
+        else:
+            p = rows_of(c * 32, 32)
+            h = tab[layer, 1 + c // 2, 1 + c % 2]
+        m = msum[p, :].astype(BF)
         z1 = dot(h, nw1[layer, 0:D, :]) + dot(m, nw1[layer, D : 2 * D, :]) + nb1[layer : layer + 1, :]
         c1, slope1 = silu_parts(0.5 * z1)
         c1 = c1.astype(BF)
@@ -365,11 +419,15 @@
         mid = z3 - jnp.mean(z3, -1, keepdims=True)
         inverse = lax.rsqrt(jnp.mean(mid * mid, -1, keepdims=True) + EPS)
         normed = mid * inverse
-        nm[layer], nc1[layer], nc2[layer] = m, c1, c2
-        nsl1[layer], nsl2[layer], nnorm[layer] = slope1, slope2, normed
-        ninv[layer] = jnp.broadcast_to(inverse, (PARTS, D))
+        nm[layer, p], nc1[layer, p], nc2[layer, p] = m, c1, c2
+        nsl1[layer, p], nsl2[layer, p], nnorm[layer, p] = slope1, slope2, normed
+        ninv[layer, p] = jnp.broadcast_to(inverse, h.shape)
         update = normed * ngain[layer : layer + 1, :] + nshift[layer : layer + 1, :]
-        return (h.astype(F32) + update).astype(BF)
+        result = (h.astype(F32) + update).astype(BF)
+        if c is None:
+            nodes_out[...] = result
+        else:
+            tab[1, 1 + c // 2, 1 + c % 2] = result
 
     def node_backward(layer, h, gh, dst, row, vec):
         normed = nnorm[layer]
@@ -419,7 +477,8 @@
             low2 = [g.astype(BF) for g in g2]
             low1 = [(dot(g, w2t[layer]) * s1[s, :].astype(F32)).astype(BF) for s, g in zip(groups, low2)]
             for s, g, f in zip(groups, low1, firsts):
-                ge[s, :] = f[0] + dot(g, w1et[layer])
+                ge[s, :] = f[0]
+                s1[s, :] = g
             sums[layer, 0] += sum(partial_rows(f[3]) for f in firsts)
             sums[layer, 1] += sum(partial_rows(f[1]) for f in firsts)
             sums[layer, 2] += sum(partial_rows(g) for g in g3)
@@ -427,21 +486,44 @@
             s = rows_of(t * CELL, CELL)
             left = jnp.concatenate([onehot[s, :], e_in[s, :]], 1)
             tt[layer, t] = dot_tn(jnp.concatenate(low1, 0), left)
-            dw2[layer] += dot_tn(jnp.concatenate(low2, 0), a1[s, :])
-            dw3[layer] += dot_tn(jnp.concatenate(low3, 0), a2[s, :])
-            if layer == 0:
-                pltpu.make_async_copy(ge.at[s], grad_edges.at[s], out_sem.at[1, t]).start()
-
-                @pl.when(t == 1)
+            if layer == 1:
+                for s, two, three in zip(groups, low2, low3):
+                    s2[s, :] = two
+                    nn[s, :] = three
+            else:
+                dw2[layer] += dot_tn(jnp.concatenate(low2, 0), a1[s, :])
+                dw3[layer] += dot_tn(jnp.concatenate(low3, 0), a2[s, :])
+
+                @pl.when(t == 0)
                 def _():
                     sum1.scatter_finish()
                     sum1.column_start()
 
-                @pl.when(t == 3)
+                @pl.when(t == 1)
                 def _():
+                    sumn.scatter_finish()
+                    sumn.column_start()
                     sum1.column_finish()
                     sum1.gather_start()
 
+                @pl.when(t == 2)
+                def _():
+                    sumn.column_finish()
+                    sumn.gather_start()
+
+            return carry
+
+        lax.fori_loop(0, 4, body, 0)
+
+    def backward_rest(layer):
+        a1, s1, a2, s2, nn, rr = kept[layer]
+
+        def body(t, carry):
+            s = rows_of(t * CELL, CELL)
+            ge[s, :] += dot(s1[s, :], w1et[layer])
+            if layer == 1:
+                dw2[layer] += dot_tn(s2[s, :], a1[s, :])
+                dw3[layer] += dot_tn(nn[s, :], a2[s, :])
             return carry
 
         lax.fori_loop(0, 4, body, 0)
@@ -517,72 +599,82 @@
             block = jnp.where(at == k, v, block)
         dst[row : row + 16, :] = block.astype(BF)
 
-    halo_finish(0)
-    prepare(0)
+    halo_finish()
+    prepare(0, (0, 1, 2, 3))
     forward(0)
-    h1 = node_forward(0, nodes[...])
-    halo_start(1, h1)
-    halo_finish(1)
-    prepare(1)
+    node_forward(0, 3)
+    cell_start(3)
+    cells_arrive(FIRST_HALO)
+    prepare(1, (3,))
     forward(1)
-    own1 = jnp.concatenate([tab[1, 1 + c // 2, 1 + c % 2] for c in range(4)], 0)
-    nodes_out[...] = node_forward(1, own1)
-
-    vec1 = []
+    node_forward(1)
+    for c in range(4):
+        for k in range(3):
+            cell_copy(c, k).wait_send()
+
+    vec1, vec0 = [], []
     gh_buf[...] = ct_nodes[...].astype(F32)
     src1[VEC1 + 16 :, :] = jnp.zeros((CH1 * 16 - VEC1 - 16, D), BF)
     src0[VEC0 + 16 :, :] = jnp.zeros((CH0 * 16 - VEC0 - 16, D), BF)
+    own1 = jnp.concatenate([tab[1, 1 + c // 2, 1 + c % 2] for c in range(4)], 0)
     node_backward(1, own1, gh_buf[...], src1, NODE_W1, vec1)
     backward(1)
     rims_start(1)
+    backward_rest(1)
     edge_grads(1, own1, src1, EDGE_W1, vec1)
-    gh_buf[...] = rims_finish(1, gh_buf[...])
-
-    node_backward(0, nodes[...], gh_buf[...], src1, NODE0, vec1)
     put_vectors(src1, VEC1, vec1)
     sum1.scatter_start()
+    gh_buf[...] = rims_finish(1, gh_buf[...])
+
+    node_backward(0, nodes[...], gh_buf[...], srcn, 0, vec0)
+    sumn.scatter_start()
     backward(0)
     rims_start(0)
-    vec0 = []
     edge_grads(0, nodes[...], src0, EDGE_W1, vec0)
     put_vectors(src0, VEC0, vec0)
     sum0.scatter_start()
+    backward_rest(0)
     grad_nodes[...] = rims_finish(0, gh_buf[...])
     sum0.scatter_finish()
     sum0.column_start()
     sum1.gather_finish()
+    sumn.gather_finish()
     sum0.column_finish()
     sum0.gather_start()
+    sum0.gather_finish()
+
+
+def unpack_kernel(nodes_in, edges_in, grad_nodes_in, grad_edges_in, sum1, sumn, sum0, *rest):
+    (nodes_out, edges_out, grad_nodes, grad_edges), outs, sems = rest[:4], rest[4:20], rest[20]
+    w1, b1, w2, b2, w3, b3, gain, shift, v1, c1, v2, c2, v3, c3, ngain, nshift = outs
+    copies = []
     for t in range(4):
-        s = rows_of(t * CELL, CELL)
-        pltpu.make_async_copy(e2.at[s], edges_out.at[s], out_sem.at[0, t]).wait()
-        pltpu.make_async_copy(ge.at[s], grad_edges.at[s], out_sem.at[1, t]).wait()
-    sum0.gather_finish()
-
-
-def unpack_kernel(sum1, sum0, *outs):
-    w1, b1, w2, b2, w3, b3, gain, shift, v1, c1, v2, c2, v3, c3, ngain, nshift = outs
+        s = pl.ds(t * CELL, CELL)
+        copies.append(pltpu.make_async_copy(grad_edges_in.at[s], grad_edges.at[s], sems.at[0, t]))
+        copies.append(pltpu.make_async_copy(edges_in.at[s], edges_out.at[s], sems.at[1, t]))
+    for copy in copies:
+        copy.start()
+    nodes_out[...] = nodes_in[...]
+    grad_nodes[...] = grad_nodes_in[...]
 
     def put(ref, layer, buffer, row):
         height = ref.shape[1]
         ref[layer] = buffer[row : row + height, :].astype(F32)
 
-    for layer, buffer, row in ((1, sum1, 0), (0, sum0, 0)):
-        put(w1, layer, buffer, row + EDGE_W1)
-        put(w2, layer, buffer, row + EDGE_W2)
-        put(w3, layer, buffer, row + EDGE_W3)
-    for layer, row in ((1, 0), (0, NODE0 - NODE_W1)):
-        put(v1, layer, sum1, row + NODE_W1)
-        put(v2, layer, sum1, row + NODE_W2)
-        put(v3, layer, sum1, row + NODE_W3)
-    first = sum1[VEC1 : VEC1 + 16, :].astype(F32)
-    second = sum0[VEC0 : VEC0 + 16, :].astype(F32)
-    for k, ref in enumerate((c1, c2, c3, ngain, nshift)):
-        ref[1:2, :] = first[k : k + 1]
-        ref[0:1, :] = first[10 + k : 11 + k]
-    for k, ref in enumerate((b1, b2, b3, gain, shift)):
-        ref[1:2, :] = first[5 + k : 6 + k]
-        ref[0:1, :] = second[k : k + 1]
+    for layer, buffer in ((1, sum1), (0, sum0)):
+        put(w1, layer, buffer, EDGE_W1)
+        put(w2, layer, buffer, EDGE_W2)
+        put(w3, layer, buffer, EDGE_W3)
+    for layer, buffer, row in ((1, sum1, 0), (0, sumn, -NODE_W1)):
+        put(v1, layer, buffer, row + NODE_W1)
+        put(v2, layer, buffer, row + NODE_W2)
+        put(v3, layer, buffer, row + NODE_W3)
+    for layer, block in ((1, sum1[VEC1 : VEC1 + 16, :]), (0, sum0[VEC0 : VEC0 + 16, :])):
+        rows = block.astype(F32)
+        for k, ref in enumerate((c1, c2, c3, ngain, nshift, b1, b2, b3, gain, shift)):
+            ref[layer : layer + 1, :] = rows[k : k + 1]
+    for copy in copies:
+        copy.wait()
 
 
 def per_device(nodes, edges, nbr_index, nbr_mask, *rest):
@@ -605,9 +697,8 @@
 
     scratch = [
         pltpu.VMEM((ROWS, 3 * D), BF),
-        big, big, big, big,
+        big, big, big,
         *([big] * 12),
-        pltpu.VMEM((ROWS, D), F32),
         pltpu.VMEM((PARTS, D), F32),
         pltpu.VMEM((2, 4, 4, 32, D), BF),
         pltpu.VMEM((4, 4 * D, D), BF),
@@ -627,25 +718,27 @@
         pltpu.VMEM((PARTS, D), BF),
         pltpu.VMEM((PARTS, D), F32),
         *sum_scratch(CH1),
+        *sum_scratch(CHN),
         *sum_scratch(CH0),
-        dma((2, 4)), dma((2, 4)), dma((2, 8)), dma((2, 8)), dma((2, 8)), dma((2, 8)),
-        *([dma((15,)), dma((16,)), dma((7,)), dma((8,)), dma((15,)), dma((16,))] * 2),
+        dma((2, 4)), dma((8,)), dma((8,)), dma((4, 3)), dma((4, 4)), dma((2, 8)), dma((2, 8)),
+        *([dma((15,)), dma((16,)), dma((7,)), dma((8,)), dma((15,)), dma((16,))] * 3),
     ]
-    nodes_out, edges_out, grad_nodes, grad_edges, sum1, sum0 = pl.pallas_call(
+    held = pl.pallas_call(
         main_kernel,
         out_shape=(
-            shape((PARTS, D), BF),
-            shape((ROWS, D), BF),
-            shape((PARTS, D), F32),
-            shape((ROWS, D), F32),
-            shape((16 * CH1, D), BF),
-            shape((16 * CH0, D), BF),
+            pltpu.VMEM((PARTS, D), BF),
+            pltpu.VMEM((ROWS, D), BF),
+            pltpu.VMEM((PARTS, D), F32),
+            pltpu.VMEM((ROWS, D), F32),
+            pltpu.VMEM((16 * CH1, D), BF),
+            pltpu.VMEM((16 * CHN, D), BF),
+            pltpu.VMEM((16 * CH0, D), BF),
         ),
         in_specs=[vmem, hbm] + [vmem] * 19 + [hbm],
-        out_specs=(vmem, hbm, vmem, hbm, vmem, vmem),
+        out_specs=(vmem,) * 7,
         scratch_shapes=scratch,
         compiler_params=pltpu.CompilerParams(
-            collective_id=0, has_side_effects=True, vmem_limit_bytes=60 * 1024 * 1024
+            collective_id=0, has_side_effects=True, vmem_limit_bytes=48 * 1024 * 1024
         ),
         name="interaction_layers",
     )(
@@ -657,13 +750,22 @@
         ct_nodes.reshape(PARTS, D),
         ct_edges.reshape(ROWS, D),
     )
-    grads = pl.pallas_call(
+    held = [pltpu.with_memory_space_constraint(value, pltpu.VMEM) for value in held]
+    nodes_out, edges_out, grad_nodes, grad_edges, *grads = pl.pallas_call(
         unpack_kernel,
-        out_shape=tuple(shape(w.shape, F32) for w in weights),
-        in_specs=[vmem, vmem],
-        out_specs=(vmem,) * 16,
+        out_shape=(
+            shape((PARTS, D), BF),
+            shape((ROWS, D), BF),
+            shape((PARTS, D), F32),
+            shape((ROWS, D), F32),
+            *(shape(w.shape, F32) for w in weights),
+        ),
+        in_specs=[vmem] * 7,
+        out_specs=(vmem, hbm, vmem, hbm) + (vmem,) * 16,
+        scratch_shapes=[dma((2, 4))],
+        compiler_params=pltpu.CompilerParams(vmem_limit_bytes=8 * 1024 * 1024),
         name="unpack_sums",
-    )(sum1, sum0)
+    )(*held)
     return (
         nodes_out.reshape(nodes.shape),
         edges_out.reshape(edges.shape),

time: 96.8 us -> 84.4 us (0.87)
  local copies, waits for them, and re-layouts: 7.29 us -> 0 us
  Pallas kernels: 88.4 us -> 82.9 us
    unnamed x8 -> x0, local copies, waits for them, and re-layouts: 7.29 us -> none
    pallas_call x2, Pallas kernels: 88.4 us -> 82.9 us  [the longest x1 79.1 us: per_device(): pl.pallas_call(main_kernel, out_shape=(pltpu.VMEM((PARTS, D), BF), pltpu....]
where the time goes in v1:
time: 84.4 us; the launch traced here: 83.7 us
  Pallas kernels  82.9 us (98%)
    pallas_call x1, Pallas kernels, per_device(): pl.pallas_call(main_kernel, out_shape=(pltpu.VMEM((PARTS, D), BF), pltpu....  79.1 us
    pallas_call x1, Pallas kernels, per_device(): pl.pallas_call(unpack_kernel, out_shape=(shape((PARTS, D), BF), shape((RO...  3.8 us

profile of v1, /device:TPU:0, one launch (start us, length us, event | category | flops | bytes accessed | tf_op | source)
XLA Modules:
  0.0 83.7 jit_solution(10723977046935808877)
XLA Ops:
  0.7 79.1 %interaction_layers.1 = (bf16[128,128]{1,0:T(8,128)(2,1)S(1)}, bf16[8192,128]{1,0:T(8,128)(2,1)S(1)}, f32[128,128]{1,0:T(8,128)S(1)}, f32[8192,128]{1,0:T(8,128)...) custom-call(bf16[128,128]{1,0:T(8,128)(2,1)} %bitcast.14, ...), custom_call_target="tpu_custom_call" | custom-call | tf_op jit(solution)/shard_map/interaction_layers/pallas_call | solution.py:726
  79.8 3.8 %unpack_sums.1 = (bf16[128,128]{1,0:T(8,128)(2,1)}, bf16[8192,128]{1,0:T(8,128)(2,1)}, f32[128,128]{1,0:T(8,128)}, f32[8192,128]{1,0:T(8,128)}, f32[2,384,128]{2...) custom-call(bf16[128,128]{1,0:T(8,128)(2,1)S(1)} %get-tuple-element., ...), custom_call_target="tpu_custom_call" | custom-call | tf_op jit(solution)/shard_map/unpack_sums/pallas_call | solution.py:754

commit v2 on v1

v2 whole, which is shorter than its diff:
```python
import functools

import jax
import jax.numpy as jnp
from jax import lax
from jax.experimental import pallas as pl
from jax.experimental.pallas import tpu as pltpu
from jax.sharding import PartitionSpec as P

EPS = 1e-05
BF = jnp.bfloat16
F32 = jnp.float32
MESH = pl.DeviceIdType.MESH

D = 128
ROWS = 8192
CELL = 2048
SUB = 4
PARTS = 128

DIRS = tuple((dx, dy) for dx in (-1, 0, 1) for dy in (-1, 0, 1) if (dx, dy) != (0, 0))
PLANE = tuple((dx, dy) for dx in range(4) for dy in range(4) if (dx, dy) != (0, 0))
COLUMN = tuple((dz, dg) for dz in range(2) for dg in range(4) if (dz, dg) != (0, 0))

CH1 = 80
CHN = 32
CH0 = 48
EDGE_W1, EDGE_W2, EDGE_W3 = 0, 384, 512
NODE_W1, NODE_W2, NODE_W3 = 640, 896, 1024
VEC1 = 1152
VEC0 = 640


def dot(a, b):
    return jnp.dot(a, b, preferred_element_type=F32)


def dot_nt(a, b):
    return lax.dot_general(a, b, (((1,), (1,)), ((), ())), preferred_element_type=F32)


def dot_tn(a, b):
    return lax.dot_general(a, b, (((0,), (0,)), ((), ())), preferred_element_type=F32)


def iota(shape, dim):
    return lax.broadcasted_iota(jnp.int32, shape, dim)


def silu_parts(half):
    wide = 1.0 + jnp.tanh(half)
    act = half * wide
    slope = wide * (0.5 + half - 0.5 * act)
    return act, slope


def rows_of(start, count):
    if isinstance(start, int):
        return slice(start, start + count)
    return pl.ds(pl.multiple_of(start, count), count)


def partial_rows(x):
    return jnp.sum(x.reshape(-1, 8, D), 0)


def column_sum(x):
    return jnp.sum(x, 0, keepdims=True)


def span(step, low, high, both):
    return low if step < 0 else (high if step > 0 else both)


def drain(view, sem):
    pltpu.make_async_copy(view, view, sem).wait()


class Sum:
    def __init__(self, chunk, refs, place):
        self.chunk = chunk
        self.src, self.part, self.col, self.out = refs[:4]
        self.sems = refs[4]
        self.gx, self.gy = place
        self.x, self.z, self.y = self.gx // 8, (self.gx // 4) % 2, self.gx % 4
        self.me = self.x * 4 + self.y
        self.mine = self.z * 4 + self.gy

    def rows(self, index):
        return pl.ds(pl.multiple_of(index * self.chunk, 16), self.chunk)

    def send(self, src, dst, phase, device):
        pltpu.make_async_remote_copy(
            src_ref=src,
            dst_ref=dst,
            send_sem=self.sems.at[phase, 0],
            recv_sem=self.sems.at[phase, 1],
            device_id=device,
            device_id_type=MESH,
        ).start()

    def wait(self, view, phase):
        drain(view, self.sems.at[phase, 0])
        drain(view, self.sems.at[phase, 1])

    def scatter_start(self):
        for dx, dy in PLANE:
            px, py = (self.x + dx) % 4, (self.y + dy) % 4
            src = self.src.at[self.rows(px * 4 + py)]
            self.send(src, self.part.at[self.me], 0, ((px * 2 + self.z) * 4 + py, self.gy))
        self.part[self.me] = self.src[self.rows(self.me), :]

    def scatter_finish(self):
        self.wait(self.part.at[pl.ds(0, 15)], 0)
        total = self.part[0].astype(F32)
        for k in range(1, 16):
            total = total + self.part[k].astype(F32)
        self.col[self.mine] = total.astype(BF)

    def column_start(self):
        own = self.col.at[self.mine]
        for dz, dg in COLUMN:
            pz, pg = (self.z + dz) % 2, (self.gy + dg) % 4
            self.send(own, own, 1, ((self.x * 2 + pz) * 4 + self.y, pg))

    def column_finish(self):
        self.wait(self.col.at[pl.ds(0, 7)], 1)
        total = self.col[0].astype(F32)
        for k in range(1, 8):
            total = total + self.col[k].astype(F32)
        self.out[self.rows(self.me), :] = total.astype(BF)

    def gather_start(self):
        own = self.out.at[self.rows(self.me)]
        for dx, dy in PLANE:
            px, py = (self.x + dx) % 4, (self.y + dy) % 4
            self.send(own, own, 2, ((px * 2 + self.z) * 4 + py, self.gy))

    def gather_finish(self):
        self.wait(self.out.at[pl.ds(0, 15 * self.chunk)], 2)


def main_kernel(*refs):
    (
        nodes_hbm, edges, index_hbm, mask_hbm, *weights_hbm,
    ) = refs[:20]
    ct_nodes_hbm, ct_edges = refs[20:22]
    (
        nodes_out, e2, grad_nodes, ge, sum1_out, sumn_out, sum0_out,
        index, mask,
        ew1, eb1, ew2, eb2, ew3, eb3, egain, eshift,
        nw1, nb1, nw2, nb2, nw3, nb3, ngain, nshift,
        ct_nodes,
        onehot, e0, e1, ct,
        a1_0, s1_0, a2_0, s2_0, n_0, r_0,
        a1_1, s1_1, a2_1, s2_1, n_1, r_1,
        live_count,
        tab, wbig, w2half, w3mid, w1et, w2t, w3t, averager,
        msum, gm, tt, dw2, dw3, sums,
        sender_sum, sender_low, receiver_sum, rim_in,
        nm, nc1, nc2, nsl1, nsl2, nnorm, ninv, gz, gh_buf,
        src1, part1, col1, srcn, partn, coln, src0, part0, col0,
        slot_mask, fixed,
        in_sem, weight_sem, halo_sem, cell_send, cell_recv, rim_sem,
        *sum_sems,
    ) = refs[22:]
    gx, gy = lax.axis_index("gx"), lax.axis_index("gy")
    sum1 = Sum(CH1, (src1, part1, col1, sum1_out, sum_sems[0]), (gx, gy))
    sumn = Sum(CHN, (srcn, partn, coln, sumn_out, sum_sems[1]), (gx, gy))
    sum0 = Sum(CH0, (src0, part0, col0, sum0_out, sum_sems[2]), (gx, gy))
    kept = ((a1_0, s1_0, a2_0, s2_0, n_0, r_0), (a1_1, s1_1, a2_1, s2_1, n_1, r_1))
    edge_in = (e0, e1, e2)

    def neighbour(dx, dy):
        return (gx + dx, gy + dy)

    def inside(dx, dy):
        there = None
        for step_, at, last in ((dx, gx, 31), (dy, gy, 3)):
            if step_:
                here = at > 0 if step_ < 0 else at < last
                there = here if there is None else there & here
        return there

    def when(there, act):
        pl.when(there)(act)

    tab[...] = jnp.zeros_like(tab)
    rim_in[...] = jnp.zeros_like(rim_in)
    barrier = pltpu.get_barrier_semaphore()

    def greet(device):
        pl.semaphore_signal(barrier, inc=1, device_id=device, device_id_type=MESH)

    for dx, dy in DIRS:
        when(inside(dx, dy), functools.partial(greet, neighbour(dx, dy)))
    x, z, y = sum1.x, sum1.z, sum1.y
    for dx, dy in PLANE:
        greet((((x + dx) % 4 * 2 + z) * 4 + (y + dy) % 4, gy))
    for dz, dg in COLUMN:
        greet(((x * 2 + (z + dz) % 2) * 4 + y, (gy + dg) % 4))

    def load(ref, scratch, which, t):
        s = rows_of(t * CELL, CELL)
        return pltpu.make_async_copy(ref.at[s], scratch.at[s], in_sem.at[which, t])

    own_cells = [tab.at[0, 1 + c // 2, 1 + c % 2] for c in range(4)]
    node_loads = [
        pltpu.make_async_copy(nodes_hbm.at[32 * c : 32 * c + 32], own_cells[c], in_sem.at[2, c])
        for c in range(4)
    ]
    weights = (
        ew1, eb1, ew2, eb2, ew3, eb3, egain, eshift, nw1, nb1, nw2, nb2, nw3, nb3, ngain, nshift,
    )
    small_loads = [
        pltpu.make_async_copy(src, dst, weight_sem.at[k])
        for k, (src, dst) in enumerate(
            zip((index_hbm, mask_hbm, ct_nodes_hbm, *weights_hbm), (index, mask, ct_nodes, *weights))
        )
    ]
    for copy in node_loads + small_loads:
        copy.start()
    for t in range(4):
        load(edges, e0, 0, t).start()
    nx = (gx > 0).astype(jnp.int32) + (gx < 31).astype(jnp.int32)
    ny = (gy > 0).astype(jnp.int32) + (gy < 3).astype(jnp.int32)
    pl.semaphore_wait(barrier, nx + ny + nx * ny + len(PLANE) + len(COLUMN))
    for copy in node_loads:
        copy.wait()

    def halo_copy(k):
        dx, dy = DIRS[k]
        src = tab.at[0, span(dx, 1, 2, pl.ds(1, 2)), span(dy, 1, 2, pl.ds(1, 2))]
        dst = tab.at[0, span(dx, 3, 0, pl.ds(1, 2)), span(dy, 3, 0, pl.ds(1, 2))]
        return pltpu.make_async_remote_copy(
            src_ref=src,
            dst_ref=dst,
            send_sem=halo_sem.at[0, k],
            recv_sem=halo_sem.at[1, k],
            device_id=neighbour(dx, dy),
            device_id_type=MESH,
        )

    def exchange_start(copy_of):
        for k, (dx, dy) in enumerate(DIRS):
            when(inside(dx, dy), lambda k=k: copy_of(k).start())

    def exchange_finish(copy_of):
        for k, (dx, dy) in enumerate(DIRS):
            when(inside(-dx, -dy), lambda k=k: copy_of(k).wait_recv())
            when(inside(dx, dy), lambda k=k: copy_of(k).wait_send())

    def cell_copies(c):
        i, j = c // 2, c % 2
        for k, (dx, dy) in enumerate(((2 * i - 1, 0), (0, 2 * j - 1), (2 * i - 1, 2 * j - 1))):
            a = 3 - 3 * i if dx else 1 + i
            b = 3 - 3 * j if dy else 1 + j
            copy = pltpu.make_async_remote_copy(
                src_ref=tab.at[1, 1 + i, 1 + j],
                dst_ref=tab.at[1, a, b],
                send_sem=cell_send.at[c, k],
                recv_sem=cell_recv.at[a, b],
                device_id=neighbour(dx, dy),
                device_id_type=MESH,
            )
            yield dx, dy, copy

    def cell_start(c):
        for dx, dy, copy in cell_copies(c):
            when(inside(dx, dy), copy.start)

    def cells_sent():
        for c in range(4):
            for dx, dy, copy in cell_copies(c):
                when(inside(dx, dy), copy.wait_send)

    def cells_arrive(group):
        views = {
            1: ((1, 0, ((3, 1), (3, 2))), (0, 1, ((1, 3), (2, 3))), (1, 1, ((3, 3),))),
            2: ((0, -1, ((1, 0), (2, 0))), (1, -1, ((3, 0),))),
            3: ((-1, 0, ((0, 1), (0, 2))), (-1, -1, ((0, 0),)), (-1, 1, ((0, 3),))),
        }[group]

        def wait(places):
            for a, b in places:
                drain(tab.at[1, a, b], cell_recv.at[a, b])

        for dx, dy, places in views:
            when(inside(dx, dy), functools.partial(wait, places))

    exchange_start(halo_copy)
    for t in range(4):
        load(ct_edges, ct, 1, t).start()
    for copy in small_loads:
        copy.wait()

    def latents(layer, cells=(0, 1, 2, 3)):
        return jnp.concatenate([tab[layer, 1 + c // 2, 1 + c % 2] for c in cells], 0)

    averager[...] = jnp.full((D, D), 1.0 / D, BF)
    for layer in range(2):
        w2half[layer] = (0.5 * ew2[layer].astype(F32)).astype(BF)
        w3 = ew3[layer].astype(F32)
        w3mid[layer] = (w3 - jnp.mean(w3, -1, keepdims=True)).astype(BF)
        w3t[layer] = ew3[layer].T
        w2t[layer] = ew2[layer].T
        w1et[layer] = ew1[layer, 2 * D : 3 * D, :].T
    sums[...] = jnp.zeros_like(sums)
    dw2[...] = jnp.zeros_like(dw2)
    dw3[...] = jnp.zeros_like(dw3)

    count = jnp.sum(mask[...].astype(F32), -1, keepdims=True)
    live_count[...] = jnp.broadcast_to(count, (PARTS, D))
    cell_of = iota((PARTS, 64), 0) // 32
    place = index[...] - (cell_of // 2) * 128 - (cell_of % 2) * 32
    place = (place // 128) * 96 + place % 128
    dead = mask[...] == 0
    high = jnp.where(dead, 127, place // 16)
    low = jnp.where(dead, 0, place % 16)
    digits = jnp.concatenate([high, low], 1).astype(F32).astype(BF)
    spread = jnp.where(iota((D, D), 0) < 64, 16.0, 1.0).astype(BF)
    row = iota((CELL, D), 0)
    lane = iota((CELL, D), 1)
    pick = jnp.where(lane == row // 64, 1.0, 0.0).astype(BF)
    slot_mask[...] = jnp.where(lane % 64 == row % 64, 1.0, 0.0)
    fixed[...] = jnp.where((lane == 32 + row // 64) | (lane == 64) | (lane == 65), 1.0, 0.0)
    for c in range(4):
        digits_of = jnp.concatenate([digits[32 * c : 32 * c + 32], jnp.zeros((96, D), BF)], 0)
        for g in range(4):
            at = slice(512 * g, 512 * g + 512)
            own = (dot(pick[at], digits_of) * slot_mask[at, :]).astype(BF)
            found = dot(own, spread)
            s = slice(c * CELL + 512 * g, c * CELL + 512 * g + 512)
            column = iota((512, D), 1).astype(F32)
            onehot[s, 0:128] = jnp.where(found == column, 1.0, 0.0).astype(BF)
            onehot[s, 128:256] = jnp.where(found == column + 128.0, 1.0, 0.0).astype(BF)
            onehot[s, 256:384] = jnp.where(found == column + 256.0, 1.0, fixed[at, :]).astype(BF)

    def prepare(layer, cells):
        a0, b0 = min(c // 2 for c in cells), min(c % 2 for c in cells)
        high_a, high_b = max(c // 2 for c in cells) + 3 - a0, max(c % 2 for c in cells) + 3 - b0
        region = tab[layer, a0 : a0 + high_a, b0 : b0 + high_b].reshape(high_a * high_b * 32, D)
        senders = (0.5 * dot(region, ew1[layer, D : 2 * D, :])).astype(BF).reshape(high_a, high_b, 32, D)
        receivers = (0.5 * dot(latents(layer, cells), ew1[layer, 0:D, :])).astype(BF)
        bias = 0.5 * eb1[layer : layer + 1, :]
        bias_high = bias.astype(BF).astype(F32)
        at = iota((64, D), 0)
        bias_rows = jnp.where(at == 0, bias_high, jnp.where(at == 1, bias - bias_high, 0.0)).astype(BF)
        edge_rows = (0.5 * ew1[layer, 2 * D : 3 * D, :].astype(F32)).astype(BF)
        for k, c in enumerate(cells):
            i, j = c // 2 - a0, c % 2 - b0
            for a in range(3):
                wbig[c, 96 * a : 96 * a + 96, :] = senders[i + a, j : j + 3].reshape(96, D)
            wbig[c, 288:320, :] = receivers[32 * k : 32 * k + 32]
            wbig[c, 320:384, :] = bias_rows
            wbig[c, 384:512, :] = edge_rows

    step = CELL // SUB
    per = step // 64

    def live_of(p):
        slot = iota((per, 64, D), 1).astype(F32)
        return slot < live_count[p, :][:, None, :]

    def forward(layer, c, parts=tuple(range(SUB))):
        a1, s1, a2, s2, nn, rr = kept[layer]
        e_in, e_out = edge_in[layer], edge_in[layer + 1]
        b2 = 0.5 * eb2[layer : layer + 1, :]
        b3 = eb3[layer : layer + 1, :]
        b3 = b3 - jnp.mean(b3, -1, keepdims=True)
        gain, shift = egain[layer : layer + 1, :], eshift[layer : layer + 1, :]
        groups = [rows_of(c * CELL + g * step, step) for g in parts]
        ones = [dot(jnp.concatenate([onehot[s, :], e_in[s, :]], 1), wbig[c]) for s in groups]
        first = []
        for s, half in zip(groups, ones):
            act, slope = silu_parts(half)
            a1[s, :] = act.astype(BF)
            s1[s, :] = slope.astype(BF)
            first.append(act.astype(BF))
        twos = [dot(act, w2half[layer]) + b2 for act in first]
        second = []
        for s, half in zip(groups, twos):
            act, slope = silu_parts(half)
            a2[s, :] = act.astype(BF)
            s2[s, :] = slope.astype(BF)
            second.append(act.astype(BF))
        mids = [dot(act, w3mid[layer]) + b3 for act in second]
        spreads = [dot((mid * mid).astype(BF), averager[...]) for mid in mids]
        for g, s, mid, var in zip(parts, groups, mids, spreads):
            inverse = lax.rsqrt(var + EPS)
            normed = mid * inverse
            nn[s, :] = normed.astype(BF)
            rr[s, :] = inverse
            update = (normed * gain + shift).reshape(per, 64, D)
            p = rows_of(c * 32 + g * per, per)
            live = live_of(p)
            new = e_in[s, :].astype(F32).reshape(per, 64, D) + jnp.where(live, update, 0.0)
            e_out[s, :] = new.astype(BF).reshape(step, D)
            msum[p, :] = jnp.sum(jnp.where(live, new, 0.0), 1)

    def node_forward(layer, cells):
        p = slice(32 * cells[0], 32 * cells[-1] + 32)
        h = latents(layer, cells)
        m = msum[p, :].astype(BF)
        z1 = dot(h, nw1[layer, 0:D, :]) + dot(m, nw1[layer, D : 2 * D, :]) + nb1[layer : layer + 1, :]
        c1, slope1 = silu_parts(0.5 * z1)
        c1 = c1.astype(BF)
        z2 = dot(c1, nw2[layer]) + nb2[layer : layer + 1, :]
        c2, slope2 = silu_parts(0.5 * z2)
        c2 = c2.astype(BF)
        z3 = dot(c2, nw3[layer]) + nb3[layer : layer + 1, :]
        mid = z3 - jnp.mean(z3, -1, keepdims=True)
        inverse = lax.rsqrt(jnp.mean(mid * mid, -1, keepdims=True) + EPS)
        normed = mid * inverse
        nm[layer, p], nc1[layer, p], nc2[layer, p] = m, c1, c2
        nsl1[layer, p], nsl2[layer, p], nnorm[layer, p] = slope1, slope2, normed
        ninv[layer, p] = jnp.broadcast_to(inverse, h.shape)
        update = normed * ngain[layer : layer + 1, :] + nshift[layer : layer + 1, :]
        result = (h.astype(F32) + update).astype(BF)
        if layer == 1:
            nodes_out[p, :] = result
        else:
            for k, c in enumerate(cells):
                tab[1, 1 + c // 2, 1 + c % 2] = result[32 * k : 32 * k + 32]

    def node_backward(layer, cells):
        p = slice(32 * cells[0], 32 * cells[-1] + 32)
        gh = gh_buf[p, :]
        normed = nnorm[layer, p]
        q = gh * ngain[layer : layer + 1, :]
        inner = q - jnp.mean(q, -1, keepdims=True) - normed * jnp.mean(q * normed, -1, keepdims=True)
        gz3 = ninv[layer, p] * inner
        gz2 = dot_nt(gz3.astype(BF), nw3[layer]) * nsl2[layer, p]
        gz1 = dot_nt(gz2.astype(BF), nw2[layer]) * nsl1[layer, p]
        gz[0, p], gz[1, p], gz[2, p] = gz1, gz2, gz3
        gm[p, :] = dot_nt(gz1.astype(BF), nw1[layer, D : 2 * D, :])

    def node_grads(layer, dst, row_, vec):
        low1, low2, low3 = (gz[k].astype(BF) for k in range(3))
        dst[row_ : row_ + 128, :] = dot_tn(latents(layer), low1).astype(BF)
        dst[row_ + 128 : row_ + 256, :] = dot_tn(nm[layer], low1).astype(BF)
        dst[row_ + 256 : row_ + 384, :] = dot_tn(nc1[layer], low2).astype(BF)
        dst[row_ + 384 : row_ + 512, :] = dot_tn(nc2[layer], low3).astype(BF)
        gh = gh_buf[...]
        vec.extend([column_sum(gz[k]) for k in range(3)])
        vec.extend([column_sum(gh * nnorm[layer]), column_sum(gh)])

    def backward(layer, c):
        a1, s1, a2, s2, nn, rr = kept[layer]
        e_in = edge_in[layer]
        gain = egain[layer : layer + 1, :]
        groups = [rows_of(c * CELL + g * step, step) for g in range(SUB)]
        firsts = []
        for g, s in enumerate(groups):
            p = rows_of(c * 32 + g * per, per)
            live = live_of(p)
            old = ct[s, :].astype(F32) if layer == 1 else ge[s, :]
            total = old.reshape(per, 64, D) + jnp.where(live, gm[p, :][:, None, :], 0.0)
            gy_ = jnp.where(live, total, 0.0).reshape(step, D)
            normed = nn[s, :].astype(F32)
            q = gy_ * gain
            qn = q * normed
            mean_q = dot(q.astype(BF), averager[...])
            mean_qn = dot(qn.astype(BF), averager[...])
            firsts.append((total.reshape(step, D), gy_, q, qn, normed, mean_q, mean_qn))
        g3 = [rr[s, :] * (f[2] - f[5] - f[4] * f[6]) for s, f in zip(groups, firsts)]
        low3 = [g.astype(BF) for g in g3]
        g2 = [dot(g, w3t[layer]) * s2[s, :].astype(F32) for s, g in zip(groups, low3)]
        low2 = [g.astype(BF) for g in g2]
        low1 = [(dot(g, w2t[layer]) * s1[s, :].astype(F32)).astype(BF) for s, g in zip(groups, low2)]
        for s, g, f in zip(groups, low1, firsts):
            ge[s, :] = f[0]
            s1[s, :] = g
        sums[layer, 0] += sum(partial_rows(f[3]) for f in firsts)
        sums[layer, 1] += sum(partial_rows(f[1]) for f in firsts)
        sums[layer, 2] += sum(partial_rows(g) for g in g3)
        sums[layer, 3] += sum(partial_rows(g) for g in g2)
        s = rows_of(c * CELL, CELL)
        left = jnp.concatenate([onehot[s, :], e_in[s, :]], 1)
        tt[layer, c] = dot_tn(jnp.concatenate(low1, 0), left)
        if layer == 1:
            for s, two, three in zip(groups, low2, low3):
                s2[s, :] = two
                nn[s, :] = three
        else:
            dw2[layer] += dot_tn(jnp.concatenate(low2, 0), a1[s, :])
            dw3[layer] += dot_tn(jnp.concatenate(low3, 0), a2[s, :])

    def backward_rest(layer, c):
        a1, s1, a2, s2, nn, rr = kept[layer]
        s = rows_of(c * CELL, CELL)
        ge[s, :] += dot(s1[s, :], w1et[layer])
        if layer == 1:
            dw2[layer] += dot_tn(s2[s, :], a1[s, :])
            dw3[layer] += dot_tn(nn[s, :], a2[s, :])

    def rim_copy(layer, k):
        dx, dy = DIRS[k]
        src = sender_low.at[layer, span(dx, 0, 3, pl.ds(1, 2)), span(dy, 0, 3, pl.ds(1, 2))]
        dst = rim_in.at[layer, k, 0] if dx != 0 and dy != 0 else rim_in.at[layer, k]
        return pltpu.make_async_remote_copy(
            src_ref=src,
            dst_ref=dst,
            send_sem=rim_sem.at[layer, 0, k],
            recv_sem=rim_sem.at[layer, 1, k],
            device_id=neighbour(dx, dy),
            device_id_type=MESH,
        )

    def rims_sum(layer):
        sender_sum[...] = jnp.zeros_like(sender_sum)
        for c in range(4):
            i, j = c // 2, c % 2
            by_row = tt[layer, c, :, 0:384].T
            for a in range(3):
                piece = by_row[96 * a : 96 * a + 96].reshape(3, 32, D)
                for b in range(3):
                    sender_sum[i + a, j + b] += piece[b]
            receiver_sum[32 * c : 32 * c + 32, :] = by_row[288:320]
            sums[layer, 4] += jnp.where(iota((8, D), 0) == 0, by_row[320:328], 0.0)
        sender_low[layer] = sender_sum[...].astype(BF)

    def edge_grads(layer, dst, row_, vec):
        dst[row_ : row_ + 128, :] = dot_tn(latents(layer), receiver_sum[...].astype(BF)).astype(BF)
        senders = dot_tn(tab[layer].reshape(512, D), sender_low[layer].reshape(512, D))
        dst[row_ + 128 : row_ + 256, :] = senders.astype(BF)
        by_edge = sum(tt[layer, c, :, 384:512] for c in range(4))
        dst[row_ + 256 : row_ + 384, :] = by_edge.T.astype(BF)
        dst[row_ + 384 : row_ + 512, :] = dw2[layer].T.astype(BF)
        dst[row_ + 512 : row_ + 640, :] = dw3[layer].T.astype(BF)
        s = [column_sum(sums[layer, k]) for k in range(5)]
        vec.extend([s[4], s[3], s[2], s[0] / egain[layer : layer + 1, :], s[1]])

    def node_share(layer):
        part = dot_nt(gz[0].astype(BF), nw1[layer, 0:D, :])
        gh_buf[...] += part + dot_nt(receiver_sum[...].astype(BF), ew1[layer, 0:D, :])

    def sender_share(layer):
        own = [sender_sum[1 + c // 2, 1 + c % 2] for c in range(4)]
        for k, (dx, dy) in enumerate(DIRS):
            cells = [
                (i, j)
                for i in ((0, 1) if dx == 0 else ((0,) if dx > 0 else (1,)))
                for j in ((0, 1) if dy == 0 else ((0,) if dy > 0 else (1,)))
            ]
            for at, (i, j) in enumerate(cells):
                own[2 * i + j] = own[2 * i + j] + rim_in[layer, k, at].astype(F32)
        own = jnp.concatenate(own, 0).astype(BF)
        return gh_buf[...] + dot_nt(own, ew1[layer, D : 2 * D, :])

    def put_vectors(dst, row_, vec):
        at = iota((16, D), 0)
        block = jnp.zeros((16, D), F32)
        for k, v in enumerate(vec):
            block = jnp.where(at == k, v, block)
        dst[row_ : row_ + 16, :] = block.astype(BF)

    exchange_finish(halo_copy)
    prepare(0, (0, 1, 2, 3))
    half = SUB // 2
    for c in range(4):
        load(edges, e0, 0, c).wait()
    forward(0, 0)
    forward(0, 1)
    node_forward(0, (0, 1))
    forward(0, 2, tuple(range(half)))
    cell_start(0)
    cell_start(1)
    forward(0, 2, tuple(range(half, SUB)))
    node_forward(0, (2,))
    forward(0, 3)
    cell_start(2)
    node_forward(0, (3,))
    cell_start(3)

    gh_buf[...] = ct_nodes[...].astype(F32)
    src1[VEC1 + 16 :, :] = jnp.zeros((CH1 * 16 - VEC1 - 16, D), BF)
    src0[VEC0 + 16 :, :] = jnp.zeros((CH0 * 16 - VEC0 - 16, D), BF)
    cells_arrive(1)
    prepare(1, (3,))
    forward(1, 3)
    cells_arrive(2)
    prepare(1, (2,))
    node_forward(1, (3,))
    node_backward(1, (3,))
    forward(1, 2)
    cells_arrive(3)
    prepare(1, (0, 1))
    cells_sent()
    node_forward(1, (2,))
    node_backward(1, (2,))
    forward(1, 1)
    node_forward(1, (1,))
    node_backward(1, (1,))
    forward(1, 0)

    for c in range(4):
        load(ct_edges, ct, 1, c).wait()
    node_forward(1, (0,))
    node_backward(1, (0,))
    for c in (3, 2, 1, 0):
        backward(1, c)
    rims_sum(1)
    exchange_start(functools.partial(rim_copy, 1))
    vec1, vec0 = [], []
    node_grads(1, src1, NODE_W1, vec1)
    for c in range(4):
        backward_rest(1, c)
    edge_grads(1, src1, EDGE_W1, vec1)
    put_vectors(src1, VEC1, vec1)
    node_share(1)
    sum1.scatter_start()
    exchange_finish(functools.partial(rim_copy, 1))
    gh_buf[...] = sender_share(1)

    node_backward(0, (0, 1, 2, 3))
    node_grads(0, srcn, 0, vec0)
    sumn.scatter_start()
    for c in range(4):
        backward(0, c)
    rims_sum(0)
    edge_grads(0, src0, EDGE_W1, vec0)
    put_vectors(src0, VEC0, vec0)
    sum0.scatter_start()
    exchange_start(functools.partial(rim_copy, 0))
    sum1.scatter_finish()
    sum1.column_start()
    sumn.scatter_finish()
    sumn.column_start()
    for c in range(4):
        backward_rest(0, c)
    node_share(0)
    sum0.scatter_finish()
    sum0.column_start()
    sum1.column_finish()
    sum1.gather_start()
    sumn.column_finish()
    sumn.gather_start()
    exchange_finish(functools.partial(rim_copy, 0))
    grad_nodes[...] = sender_share(0)
    sum0.column_finish()
    sum0.gather_start()
    sum1.gather_finish()
    sumn.gather_finish()
    sum0.gather_finish()


def unpack_kernel(nodes_in, edges_in, grad_nodes_in, grad_edges_in, sum1, sumn, sum0, *rest):
    (nodes_out, edges_out, grad_nodes, grad_edges), outs = rest[:4], rest[4:20]
    held, (sems, small) = rest[20:36], rest[36:]
    w1, b1, w2, b2, w3, b3, gain, shift, v1, c1, v2, c2, v3, c3, ngain, nshift = held
    copies = [
        pltpu.make_async_copy(nodes_in, nodes_out, sems.at[2, 0]),
        pltpu.make_async_copy(grad_nodes_in, grad_nodes, sems.at[2, 1]),
    ]
    for t in range(4):
        s = pl.ds(t * CELL, CELL)
        copies.append(pltpu.make_async_copy(grad_edges_in.at[s], grad_edges.at[s], sems.at[0, t]))
        copies.append(pltpu.make_async_copy(edges_in.at[s], edges_out.at[s], sems.at[1, t]))
    for copy in copies:
        copy.start()

    def put(ref, layer, buffer, row):
        height = ref.shape[1]
        ref[layer] = buffer[row : row + height, :].astype(F32)

    for layer, buffer in ((1, sum1), (0, sum0)):
        put(w1, layer, buffer, EDGE_W1)
        put(w2, layer, buffer, EDGE_W2)
        put(w3, layer, buffer, EDGE_W3)
    for layer, buffer, row in ((1, sum1, 0), (0, sumn, -NODE_W1)):
        put(v1, layer, buffer, row + NODE_W1)
        put(v2, layer, buffer, row + NODE_W2)
        put(v3, layer, buffer, row + NODE_W3)
    for layer, block in ((1, sum1[VEC1 : VEC1 + 16, :]), (0, sum0[VEC0 : VEC0 + 16, :])):
        rows = block.astype(F32)
        for k, ref in enumerate((c1, c2, c3, ngain, nshift, b1, b2, b3, gain, shift)):
            ref[layer : layer + 1, :] = rows[k : k + 1]
    for k, (src, dst) in enumerate(zip(held, outs)):
        copies.append(pltpu.make_async_copy(src, dst, small.at[k]))
        copies[-1].start()
    for copy in copies:
        copy.wait()


def per_device(nodes, edges, nbr_index, nbr_mask, *rest):
    weights, ct_nodes, ct_edges = rest[:16], rest[16], rest[17]
    vmem = pl.BlockSpec(memory_space=pltpu.VMEM)
    hbm = pl.BlockSpec(memory_space=pl.ANY)
    shape = jax.ShapeDtypeStruct
    big = pltpu.VMEM((ROWS, D), BF)
    node_bf = pltpu.VMEM((2, PARTS, D), BF)
    node_f32 = pltpu.VMEM((2, PARTS, D), F32)
    square = pltpu.VMEM((2, D, D), BF)
    dma = pltpu.SemaphoreType.DMA

    def sum_scratch(chunk):
        return [
            pltpu.VMEM((16 * chunk, D), BF),
            pltpu.VMEM((16, chunk, D), BF),
            pltpu.VMEM((8, chunk, D), BF),
        ]

    scratch = [
        pltpu.VMEM((PARTS, 64), jnp.int32),
        pltpu.VMEM((PARTS, 64), jnp.int32),
        *(pltpu.VMEM(w.shape, w.dtype) for w in weights),
        pltpu.VMEM((PARTS, D), BF),
        pltpu.VMEM((ROWS, 3 * D), BF),
        big, big, big,
        *(([big] * 5 + [pltpu.VMEM((ROWS, D), F32)]) * 2),
        pltpu.VMEM((PARTS, D), F32),
        pltpu.VMEM((2, 4, 4, 32, D), BF),
        pltpu.VMEM((4, 4 * D, D), BF),
        square, square, square, square, square,
        pltpu.VMEM((D, D), BF),
        pltpu.VMEM((PARTS, D), F32),
        pltpu.VMEM((PARTS, D), F32),
        pltpu.VMEM((2, 4, D, 4 * D), F32),
        pltpu.VMEM((2, D, D), F32),
        pltpu.VMEM((2, D, D), F32),
        pltpu.VMEM((2, 5, 8, D), F32),
        pltpu.VMEM((4, 4, 32, D), F32),
        pltpu.VMEM((2, 4, 4, 32, D), BF),
        pltpu.VMEM((PARTS, D), F32),
        pltpu.VMEM((2, 8, 2, 32, D), BF),
        node_bf, node_bf, node_bf, node_f32, node_f32, node_f32, node_f32,
        pltpu.VMEM((3, PARTS, D), F32),
        pltpu.VMEM((PARTS, D), F32),
        *sum_scratch(CH1),
        *sum_scratch(CHN),
        *sum_scratch(CH0),
        pltpu.VMEM((CELL, D), F32),
        pltpu.VMEM((CELL, D), F32),
        dma((3, 4)), dma((19,)), dma((2, 8)), dma((4, 3)), dma((4, 4)), dma((2, 2, 8)),
        *([dma((3, 2))] * 3),
    ]
    held = pl.pallas_call(
        main_kernel,
        out_shape=(
            pltpu.VMEM((PARTS, D), BF),
            pltpu.VMEM((ROWS, D), BF),
            pltpu.VMEM((PARTS, D), F32),
            pltpu.VMEM((ROWS, D), F32),
            pltpu.VMEM((16 * CH1, D), BF),
            pltpu.VMEM((16 * CHN, D), BF),
            pltpu.VMEM((16 * CH0, D), BF),
        ),
        in_specs=[hbm] * 22,
        out_specs=(vmem,) * 7,
        scratch_shapes=scratch,
        compiler_params=pltpu.CompilerParams(
            collective_id=0, has_side_effects=True, vmem_limit_bytes=53 * 1024 * 1024
        ),
        name="interaction_layers",
    )(
        nodes.reshape(PARTS, D),
        edges.reshape(ROWS, D),
        nbr_index.reshape(PARTS, 64),
        nbr_mask.reshape(PARTS, 64),
        *weights,
        ct_nodes.reshape(PARTS, D),
        ct_edges.reshape(ROWS, D),
    )
    held = [pltpu.with_memory_space_constraint(value, pltpu.VMEM) for value in held]
    nodes_out, edges_out, grad_nodes, grad_edges, *grads = pl.pallas_call(
        unpack_kernel,
        out_shape=(
            shape((PARTS, D), BF),
            shape((ROWS, D), BF),
            shape((PARTS, D), F32),
            shape((ROWS, D), F32),
            *(shape(w.shape, F32) for w in weights),
        ),
        in_specs=[vmem] * 7,
        out_specs=(hbm,) * 20,
        scratch_shapes=[*(pltpu.VMEM(w.shape, F32) for w in weights), dma((3, 4)), dma((16,))],
        compiler_params=pltpu.CompilerParams(vmem_limit_bytes=8 * 1024 * 1024),
        name="unpack_sums",
    )(*held)
    return (
        nodes_out.reshape(nodes.shape),
        edges_out.reshape(edges.shape),
        grad_nodes.reshape(nodes.shape),
        grad_edges.reshape(edges.shape),
        *grads,
    )


def solution(mesh):
    cells = P("gx", "gy", None, None)
    wide = P("gx", "gy", None, None, None)
    in_specs = (cells, wide, cells, cells) + (P(),) * 16 + (cells, wide)
    out_specs = (cells, wide, cells, wide) + (P(),) * 16
    return jax.shard_map(
        per_device, mesh=mesh, in_specs=in_specs, out_specs=out_specs, check_vma=False
    )
```

time: 84.4 us -> 70.2 us (0.83)
  Pallas kernels: 82.9 us -> 69.3 us
    pallas_call x1, Pallas kernels: 79.1 us -> 66 us  [per_device(): pl.pallas_call(main_kernel, out_shape=(pltpu.VMEM((PARTS, D), BF), pltpu....]
where the time goes in v2:
time: 70.2 us; the launch traced here: 70.1 us
  Pallas kernels  69.3 us (99%)
  between operations  0.86 us (1%)
    pallas_call x1, Pallas kernels, per_device(): pl.pallas_call(main_kernel, out_shape=(pltpu.VMEM((PARTS, D), BF), pltpu....  66 us
    pallas_call x1, Pallas kernels, per_device(): pl.pallas_call(unpack_kernel, out_shape=(shape((PARTS, D), BF), shape((RO...  3.32 us

profile of v2, /device:TPU:0, one launch (start us, length us, event | category | flops | bytes accessed | tf_op | source)
XLA Modules:
  0.0 70.1 jit_solution(5921572475288507576)
XLA Ops:
  0.7 66.0 %interaction_layers.1 = (bf16[128,128]{1,0:T(8,128)(2,1)S(1)}, bf16[8192,128]{1,0:T(8,128)(2,1)S(1)}, f32[128,128]{1,0:T(8,128)S(1)}, f32[8192,128]{1,0:T(8,128)...) custom-call(bf16[128,128]{1,0:T(8,128)(2,1)} %bitcast.14, ...), custom_call_target="tpu_custom_call" | custom-call | tf_op jit(solution)/shard_map/interaction_layers/pallas_call | solution.py:738
  66.6 3.3 %unpack_sums.1 = (bf16[128,128]{1,0:T(8,128)(2,1)}, bf16[8192,128]{1,0:T(8,128)(2,1)}, f32[128,128]{1,0:T(8,128)}, f32[8192,128]{1,0:T(8,128)}, f32[2,384,128]{2...) custom-call(bf16[128,128]{1,0:T(8,128)(2,1)S(1)} %get-tuple-element., ...), custom_call_target="tpu_custom_call" | custom-call | tf_op jit(solution)/shard_map/unpack_sums/pallas_call | solution.py:766

commit v3 on v2

--- a/solution.py
+++ b/solution.py
@@ -18,9 +18,11 @@
 SUB = 4
 PARTS = 128
 
-DIRS = tuple((dx, dy) for dx in (-1, 0, 1) for dy in (-1, 0, 1) if (dx, dy) != (0, 0))
-PLANE = tuple((dx, dy) for dx in range(4) for dy in range(4) if (dx, dy) != (0, 0))
-COLUMN = tuple((dz, dg) for dz in range(2) for dg in range(4) if (dz, dg) != (0, 0))
+DIRS = ((1, 0), (-1, 0), (1, 1), (-1, -1), (1, -1), (-1, 1), (0, 1), (0, -1))
+PLANE = (
+    (2, 2), (1, 2), (2, 1), (3, 2), (2, 3), (2, 0), (0, 2), (1, 1), (3, 3), (1, 3), (3, 1), (1, 0), (0, 1), (3, 0), (0, 3),
+)
+COLUMN = ((1, 0), (1, 1), (1, 3), (1, 2), (0, 2), (0, 3), (0, 1))
 
 CH1 = 80
 CHN = 32
@@ -156,11 +158,10 @@
         a1_1, s1_1, a2_1, s2_1, n_1, r_1,
         live_count,
         tab, wbig, w2half, w3mid, w1et, w2t, w3t, averager,
-        msum, gm, tt, dw2, dw3, sums,
+        msum, gm, tt, dw, sums, window,
         sender_sum, sender_low, receiver_sum, rim_in,
         nm, nc1, nc2, nsl1, nsl2, nnorm, ninv, gz, gh_buf,
         src1, part1, col1, srcn, partn, coln, src0, part0, col0,
-        slot_mask, fixed,
         in_sem, weight_sem, halo_sem, cell_send, cell_recv, rim_sem,
         *sum_sems,
     ) = refs[22:]
@@ -185,7 +186,18 @@
     def when(there, act):
         pl.when(there)(act)
 
-    tab[...] = jnp.zeros_like(tab)
+    own_cells = [tab.at[0, 1 + c // 2, 1 + c % 2] for c in range(4)]
+    node_loads = [
+        pltpu.make_async_copy(nodes_hbm.at[32 * c : 32 * c + 32], own_cells[c], in_sem.at[2, c])
+        for c in range(4)
+    ]
+    for copy in node_loads:
+        copy.start()
+    tab[1] = jnp.zeros_like(tab[1])
+    for a in range(4):
+        for b in range(4):
+            if a in (0, 3) or b in (0, 3):
+                tab[0, a, b] = jnp.zeros((32, D), BF)
     rim_in[...] = jnp.zeros_like(rim_in)
     barrier = pltpu.get_barrier_semaphore()
 
@@ -204,11 +216,6 @@
         s = rows_of(t * CELL, CELL)
         return pltpu.make_async_copy(ref.at[s], scratch.at[s], in_sem.at[which, t])
 
-    own_cells = [tab.at[0, 1 + c // 2, 1 + c % 2] for c in range(4)]
-    node_loads = [
-        pltpu.make_async_copy(nodes_hbm.at[32 * c : 32 * c + 32], own_cells[c], in_sem.at[2, c])
-        for c in range(4)
-    ]
     weights = (
         ew1, eb1, ew2, eb2, ew3, eb3, egain, eshift, nw1, nb1, nw2, nb2, nw3, nb3, ngain, nshift,
     )
@@ -218,7 +225,7 @@
             zip((index_hbm, mask_hbm, ct_nodes_hbm, *weights_hbm), (index, mask, ct_nodes, *weights))
         )
     ]
-    for copy in node_loads + small_loads:
+    for copy in small_loads:
         copy.start()
     for t in range(4):
         load(edges, e0, 0, t).start()
@@ -302,12 +309,12 @@
         w2half[layer] = (0.5 * ew2[layer].astype(F32)).astype(BF)
         w3 = ew3[layer].astype(F32)
         w3mid[layer] = (w3 - jnp.mean(w3, -1, keepdims=True)).astype(BF)
-        w3t[layer] = ew3[layer].T
+        w3t[layer] = w3mid[layer].T
         w2t[layer] = ew2[layer].T
         w1et[layer] = ew1[layer, 2 * D : 3 * D, :].T
     sums[...] = jnp.zeros_like(sums)
-    dw2[...] = jnp.zeros_like(dw2)
-    dw3[...] = jnp.zeros_like(dw3)
+    dw[...] = jnp.zeros_like(dw)
+    window[...] = jnp.zeros_like(window)
 
     count = jnp.sum(mask[...].astype(F32), -1, keepdims=True)
     live_count[...] = jnp.broadcast_to(count, (PARTS, D))
@@ -322,6 +329,7 @@
     row = iota((CELL, D), 0)
     lane = iota((CELL, D), 1)
     pick = jnp.where(lane == row // 64, 1.0, 0.0).astype(BF)
+    slot_mask, fixed = ge.at[0:CELL], ge.at[CELL : 2 * CELL]
     slot_mask[...] = jnp.where(lane % 64 == row % 64, 1.0, 0.0)
     fixed[...] = jnp.where((lane == 32 + row // 64) | (lane == 64) | (lane == 65), 1.0, 0.0)
     for c in range(4):
@@ -351,6 +359,8 @@
             i, j = c // 2 - a0, c % 2 - b0
             for a in range(3):
                 wbig[c, 96 * a : 96 * a + 96, :] = senders[i + a, j : j + 3].reshape(96, D)
+                window[layer, c, 96 * a : 96 * a + 96, 0:128] = tab[layer, c // 2 + a, c % 2 : c % 2 + 3].reshape(96, D)
+            window[layer, c, 288:320, 128:256] = tab[layer, 1 + c // 2, 1 + c % 2]
             wbig[c, 288:320, :] = receivers[32 * k : 32 * k + 32]
             wbig[c, 320:384, :] = bias_rows
             wbig[c, 384:512, :] = edge_rows
@@ -460,10 +470,9 @@
             normed = nn[s, :].astype(F32)
             q = gy_ * gain
             qn = q * normed
-            mean_q = dot(q.astype(BF), averager[...])
             mean_qn = dot(qn.astype(BF), averager[...])
-            firsts.append((total.reshape(step, D), gy_, q, qn, normed, mean_q, mean_qn))
-        g3 = [rr[s, :] * (f[2] - f[5] - f[4] * f[6]) for s, f in zip(groups, firsts)]
+            firsts.append((total.reshape(step, D), gy_, q, qn, normed, mean_qn))
+        g3 = [rr[s, :] * (f[2] - f[4] * f[5]) for s, f in zip(groups, firsts)]
         low3 = [g.astype(BF) for g in g3]
         g2 = [dot(g, w3t[layer]) * s2[s, :].astype(F32) for s, g in zip(groups, low3)]
         low2 = [g.astype(BF) for g in g2]
@@ -483,16 +492,16 @@
                 s2[s, :] = two
                 nn[s, :] = three
         else:
-            dw2[layer] += dot_tn(jnp.concatenate(low2, 0), a1[s, :])
-            dw3[layer] += dot_tn(jnp.concatenate(low3, 0), a2[s, :])
+            dw[layer, 0:128] += dot_tn(jnp.concatenate(low2, 0), a1[s, :])
+            dw[layer, 128:256] += dot_tn(jnp.concatenate(low3, 0), a2[s, :])
 
     def backward_rest(layer, c):
         a1, s1, a2, s2, nn, rr = kept[layer]
         s = rows_of(c * CELL, CELL)
         ge[s, :] += dot(s1[s, :], w1et[layer])
         if layer == 1:
-            dw2[layer] += dot_tn(s2[s, :], a1[s, :])
-            dw3[layer] += dot_tn(nn[s, :], a2[s, :])
+            dw[layer, 0:128] += dot_tn(s2[s, :], a1[s, :])
+            dw[layer, 128:256] += dot_tn(nn[s, :], a2[s, :])
 
     def rim_copy(layer, k):
         dx, dy = DIRS[k]
@@ -517,19 +526,21 @@
                 for b in range(3):
                     sender_sum[i + a, j + b] += piece[b]
             receiver_sum[32 * c : 32 * c + 32, :] = by_row[288:320]
-            sums[layer, 4] += jnp.where(iota((8, D), 0) == 0, by_row[320:328], 0.0)
         sender_low[layer] = sender_sum[...].astype(BF)
 
     def edge_grads(layer, dst, row_, vec):
-        dst[row_ : row_ + 128, :] = dot_tn(latents(layer), receiver_sum[...].astype(BF)).astype(BF)
-        senders = dot_tn(tab[layer].reshape(512, D), sender_low[layer].reshape(512, D))
-        dst[row_ + 128 : row_ + 256, :] = senders.astype(BF)
+        by_node = sum(dot(tt[layer, c, :, 0:384].astype(BF), window[layer, c]) for c in range(4))
         by_edge = sum(tt[layer, c, :, 384:512] for c in range(4))
+        ones = sum(tt[layer, c, :, 256:384] for c in range(4)).T[64:65]
+        dst[row_ : row_ + 128, :] = by_node[:, 128:256].T.astype(BF)
+        dst[row_ + 128 : row_ + 256, :] = by_node[:, 0:128].T.astype(BF)
         dst[row_ + 256 : row_ + 384, :] = by_edge.T.astype(BF)
-        dst[row_ + 384 : row_ + 512, :] = dw2[layer].T.astype(BF)
-        dst[row_ + 512 : row_ + 640, :] = dw3[layer].T.astype(BF)
-        s = [column_sum(sums[layer, k]) for k in range(5)]
-        vec.extend([s[4], s[3], s[2], s[0] / egain[layer : layer + 1, :], s[1]])
+        dst[row_ + 384 : row_ + 512, :] = dw[layer, 0:128].T.astype(BF)
+        third = dw[layer, 128:256].T
+        dst[row_ + 512 : row_ + 640, :] = (third - jnp.mean(third, -1, keepdims=True)).astype(BF)
+        s = [column_sum(sums[layer, k]) for k in range(4)]
+        s[2] = s[2] - jnp.mean(s[2], -1, keepdims=True)
+        vec.extend([ones, s[3], s[2], s[0] / egain[layer : layer + 1, :], s[1]])
 
     def node_share(layer):
         part = dot_nt(gz[0].astype(BF), nw1[layer, 0:D, :])
@@ -618,10 +629,10 @@
     sumn.scatter_start()
     for c in range(4):
         backward(0, c)
-    rims_sum(0)
     edge_grads(0, src0, EDGE_W1, vec0)
     put_vectors(src0, VEC0, vec0)
     sum0.scatter_start()
+    rims_sum(0)
     exchange_start(functools.partial(rim_copy, 0))
     sum1.scatter_finish()
     sum1.column_start()
@@ -717,9 +728,9 @@
         pltpu.VMEM((PARTS, D), F32),
         pltpu.VMEM((PARTS, D), F32),
         pltpu.VMEM((2, 4, D, 4 * D), F32),
-        pltpu.VMEM((2, D, D), F32),
-        pltpu.VMEM((2, D, D), F32),
-        pltpu.VMEM((2, 5, 8, D), F32),
+        pltpu.VMEM((2, 2 * D, D), F32),
+        pltpu.VMEM((2, 4, 8, D), F32),
+        pltpu.VMEM((2, 4, 3 * D, 2 * D), BF),
         pltpu.VMEM((4, 4, 32, D), F32),
         pltpu.VMEM((2, 4, 4, 32, D), BF),
         pltpu.VMEM((PARTS, D), F32),
@@ -730,8 +741,6 @@
         *sum_scratch(CH1),
         *sum_scratch(CHN),
         *sum_scratch(CH0),
-        pltpu.VMEM((CELL, D), F32),
-        pltpu.VMEM((CELL, D), F32),
         dma((3, 4)), dma((19,)), dma((2, 8)), dma((4, 3)), dma((4, 4)), dma((2, 2, 8)),
         *([dma((3, 2))] * 3),
     ]

time: 70.2 us -> 68.8 us (0.980)
  Pallas kernels: 69.3 us -> 67.9 us
    pallas_call x1, Pallas kernels: 66 us -> 64.6 us  [per_device(): pl.pallas_call(main_kernel, out_shape=(pltpu.VMEM((PARTS, D), BF), pltpu....]
where the time goes in v3:
time: 68.8 us; the launch traced here: 68.7 us
  Pallas kernels  67.9 us (99%)
  between operations  0.86 us (1%)
    pallas_call x1, Pallas kernels, per_device(): pl.pallas_call(main_kernel, out_shape=(pltpu.VMEM((PARTS, D), BF), pltpu....  64.6 us
    pallas_call x1, Pallas kernels, per_device(): pl.pallas_call(unpack_kernel, out_shape=(shape((PARTS, D), BF), shape((RO...  3.32 us

profile of v3, /device:TPU:0, one launch (start us, length us, event | category | flops | bytes accessed | tf_op | source)
XLA Modules:
  0.0 68.7 jit_solution(9329742000218618667)
XLA Ops:
  0.7 64.6 %interaction_layers.1 = (bf16[128,128]{1,0:T(8,128)(2,1)S(1)}, bf16[8192,128]{1,0:T(8,128)(2,1)S(1)}, f32[128,128]{1,0:T(8,128)S(1)}, f32[8192,128]{1,0:T(8,128)...) custom-call(bf16[128,128]{1,0:T(8,128)(2,1)} %bitcast.14, ...), custom_call_target="tpu_custom_call" | custom-call | tf_op jit(solution)/shard_map/interaction_layers/pallas_call | solution.py:747
  65.2 3.3 %unpack_sums.1 = (bf16[128,128]{1,0:T(8,128)(2,1)}, bf16[8192,128]{1,0:T(8,128)(2,1)}, f32[128,128]{1,0:T(8,128)}, f32[8192,128]{1,0:T(8,128)}, f32[2,384,128]{2...) custom-call(bf16[128,128]{1,0:T(8,128)(2,1)S(1)} %get-tuple-element., ...), custom_call_target="tpu_custom_call" | custom-call | tf_op jit(solution)/shard_map/unpack_sums/pallas_call | solution.py:775

commit v4 on v3

--- a/solution.py
+++ b/solution.py
@@ -18,7 +18,8 @@
 SUB = 4
 PARTS = 128
 
-DIRS = ((1, 0), (-1, 0), (1, 1), (-1, -1), (1, -1), (-1, 1), (0, 1), (0, -1))
+DIRS = ((1, 0), (1, 1), (1, -1), (0, 1), (0, -1), (-1, 0), (-1, 1), (-1, -1))
+EARLY, LATE = range(5), range(5, 8)
 PLANE = (
     (2, 2), (1, 2), (2, 1), (3, 2), (2, 3), (2, 0), (0, 2), (1, 1), (3, 3), (1, 3), (3, 1), (1, 0), (0, 1), (3, 0), (0, 3),
 )
@@ -248,14 +249,22 @@
             device_id_type=MESH,
         )
 
-    def exchange_start(copy_of):
-        for k, (dx, dy) in enumerate(DIRS):
-            when(inside(dx, dy), lambda k=k: copy_of(k).start())
-
-    def exchange_finish(copy_of):
-        for k, (dx, dy) in enumerate(DIRS):
+    def exchange_start(copy_of, directions=range(8)):
+        for k in directions:
+            when(inside(*DIRS[k]), lambda k=k: copy_of(k).start())
+
+    def exchange_finish(copy_of, directions=range(8)):
+        for k in directions:
+            dx, dy = DIRS[k]
             when(inside(-dx, -dy), lambda k=k: copy_of(k).wait_recv())
-            when(inside(dx, dy), lambda k=k: copy_of(k).wait_send())
+
+    def all_sent():
+        for copy_of in (halo_copy, functools.partial(rim_copy, 1), functools.partial(rim_copy, 0)):
+            for k, (dx, dy) in enumerate(DIRS):
+                when(inside(dx, dy), lambda copy_of=copy_of, k=k: copy_of(k).wait_send())
+        for c in range(4):
+            for dx, dy, copy in cell_copies(c):
+                when(inside(dx, dy), copy.wait_send)
 
     def cell_copies(c):
         i, j = c // 2, c % 2
@@ -276,11 +285,6 @@
         for dx, dy, copy in cell_copies(c):
             when(inside(dx, dy), copy.start)
 
-    def cells_sent():
-        for c in range(4):
-            for dx, dy, copy in cell_copies(c):
-                when(inside(dx, dy), copy.wait_send)
-
     def cells_arrive(group):
         views = {
             1: ((1, 0, ((3, 1), (3, 2))), (0, 1, ((1, 3), (2, 3))), (1, 1, ((3, 3),))),
@@ -295,7 +299,7 @@
         for dx, dy, places in views:
             when(inside(dx, dy), functools.partial(wait, places))
 
-    exchange_start(halo_copy)
+    exchange_start(halo_copy, EARLY)
     for t in range(4):
         load(ct_edges, ct, 1, t).start()
     for copy in small_loads:
@@ -312,6 +316,7 @@
         w3t[layer] = w3mid[layer].T
         w2t[layer] = ew2[layer].T
         w1et[layer] = ew1[layer, 2 * D : 3 * D, :].T
+    exchange_start(halo_copy, LATE)
     sums[...] = jnp.zeros_like(sums)
     dw[...] = jnp.zeros_like(dw)
     window[...] = jnp.zeros_like(window)
@@ -566,13 +571,15 @@
             block = jnp.where(at == k, v, block)
         dst[row_ : row_ + 16, :] = block.astype(BF)
 
-    exchange_finish(halo_copy)
-    prepare(0, (0, 1, 2, 3))
+    exchange_finish(halo_copy, EARLY)
+    prepare(0, (0, 1))
     half = SUB // 2
     for c in range(4):
         load(edges, e0, 0, c).wait()
     forward(0, 0)
     forward(0, 1)
+    exchange_finish(halo_copy, LATE)
+    prepare(0, (2, 3))
     node_forward(0, (0, 1))
     forward(0, 2, tuple(range(half)))
     cell_start(0)
@@ -597,7 +604,6 @@
     forward(1, 2)
     cells_arrive(3)
     prepare(1, (0, 1))
-    cells_sent()
     node_forward(1, (2,))
     node_backward(1, (2,))
     forward(1, 1)
@@ -647,10 +653,11 @@
     sum1.gather_start()
     sumn.column_finish()
     sumn.gather_start()
+    sum0.column_finish()
+    sum0.gather_start()
     exchange_finish(functools.partial(rim_copy, 0))
     grad_nodes[...] = sender_share(0)
-    sum0.column_finish()
-    sum0.gather_start()
+    all_sent()
     sum1.gather_finish()
     sumn.gather_finish()
     sum0.gather_finish()

time: 68.8 us -> 68.3 us (level)
  no operation moved by 1% of the time
where the time goes in v4:
time: 68.3 us; the launch traced here: 68.2 us
  Pallas kernels  67.3 us (99%)
  between operations  0.86 us (1%)
    pallas_call x1, Pallas kernels, per_device(): pl.pallas_call(main_kernel, out_shape=(pltpu.VMEM((PARTS, D), BF), pltpu....  64 us
    pallas_call x1, Pallas kernels, per_device(): pl.pallas_call(unpack_kernel, out_shape=(shape((PARTS, D), BF), shape((RO...  3.32 us

profile of v4, /device:TPU:0, one launch (start us, length us, event | category | flops | bytes accessed | tf_op | source)
XLA Modules:
  0.0 68.2 jit_solution(8369552221442478428)
XLA Ops:
  0.7 64.0 %interaction_layers.1 = (bf16[128,128]{1,0:T(8,128)(2,1)S(1)}, bf16[8192,128]{1,0:T(8,128)(2,1)S(1)}, f32[128,128]{1,0:T(8,128)S(1)}, f32[8192,128]{1,0:T(8,128)...) custom-call(bf16[128,128]{1,0:T(8,128)(2,1)} %bitcast.14, ...), custom_call_target="tpu_custom_call" | custom-call | tf_op jit(solution)/shard_map/interaction_layers/pallas_call | solution.py:754
  64.7 3.3 %unpack_sums.1 = (bf16[128,128]{1,0:T(8,128)(2,1)}, bf16[8192,128]{1,0:T(8,128)(2,1)}, f32[128,128]{1,0:T(8,128)}, f32[8192,128]{1,0:T(8,128)}, f32[2,384,128]{2...) custom-call(bf16[128,128]{1,0:T(8,128)(2,1)S(1)} %get-tuple-element., ...), custom_call_target="tpu_custom_call" | custom-call | tf_op jit(solution)/shard_map/unpack_sums/pallas_call | solution.py:782

commit v5 on v4

--- a/solution.py
+++ b/solution.py
@@ -51,10 +51,10 @@
 
 
 def silu_parts(half):
-    wide = 1.0 + jnp.tanh(half)
+    t = jnp.tanh(half)
+    wide = 1.0 + t
     act = half * wide
-    slope = wide * (0.5 + half - 0.5 * act)
-    return act, slope
+    return act, wide + act * (1.0 - t)
 
 
 def rows_of(start, count):
@@ -313,8 +313,8 @@
         w2half[layer] = (0.5 * ew2[layer].astype(F32)).astype(BF)
         w3 = ew3[layer].astype(F32)
         w3mid[layer] = (w3 - jnp.mean(w3, -1, keepdims=True)).astype(BF)
-        w3t[layer] = w3mid[layer].T
-        w2t[layer] = ew2[layer].T
+        w3t[layer] = (0.5 * w3mid[layer].astype(F32)).astype(BF).T
+        w2t[layer] = w2half[layer].T
         w1et[layer] = ew1[layer, 2 * D : 3 * D, :].T
     exchange_start(halo_copy, LATE)
     sums[...] = jnp.zeros_like(sums)
@@ -428,7 +428,7 @@
         inverse = lax.rsqrt(jnp.mean(mid * mid, -1, keepdims=True) + EPS)
         normed = mid * inverse
         nm[layer, p], nc1[layer, p], nc2[layer, p] = m, c1, c2
-        nsl1[layer, p], nsl2[layer, p], nnorm[layer, p] = slope1, slope2, normed
+        nsl1[layer, p], nsl2[layer, p], nnorm[layer, p] = 0.5 * slope1, 0.5 * slope2, normed
         ninv[layer, p] = jnp.broadcast_to(inverse, h.shape)
         update = normed * ngain[layer : layer + 1, :] + nshift[layer : layer + 1, :]
         result = (h.astype(F32) + update).astype(BF)

time: 68.3 us -> 68 us (level)
  no operation moved by 1% of the time
where the time goes in v5:
time: 68 us; the launch traced here: 67.9 us
  Pallas kernels  67.1 us (99%)
  between operations  0.86 us (1%)
    pallas_call x1, Pallas kernels, per_device(): pl.pallas_call(main_kernel, out_shape=(pltpu.VMEM((PARTS, D), BF), pltpu....  63.7 us
    pallas_call x1, Pallas kernels, per_device(): pl.pallas_call(unpack_kernel, out_shape=(shape((PARTS, D), BF), shape((RO...  3.32 us

profile of v5, /device:TPU:0, one launch (start us, length us, event | category | flops | bytes accessed | tf_op | source)
XLA Modules:
  0.0 67.9 jit_solution(15244231948090917243)
XLA Ops:
  0.7 63.7 %interaction_layers.1 = (bf16[128,128]{1,0:T(8,128)(2,1)S(1)}, bf16[8192,128]{1,0:T(8,128)(2,1)S(1)}, f32[128,128]{1,0:T(8,128)S(1)}, f32[8192,128]{1,0:T(8,128)...) custom-call(bf16[128,128]{1,0:T(8,128)(2,1)} %bitcast.14, ...), custom_call_target="tpu_custom_call" | custom-call | tf_op jit(solution)/shard_map/interaction_layers/pallas_call | solution.py:754
  64.4 3.3 %unpack_sums.1 = (bf16[128,128]{1,0:T(8,128)(2,1)}, bf16[8192,128]{1,0:T(8,128)(2,1)}, f32[128,128]{1,0:T(8,128)}, f32[8192,128]{1,0:T(8,128)}, f32[2,384,128]{2...) custom-call(bf16[128,128]{1,0:T(8,128)(2,1)S(1)} %get-tuple-element., ...), custom_call_target="tpu_custom_call" | custom-call | tf_op jit(solution)/shard_map/unpack_sums/pallas_call | solution.py:782
